TPU v7x, 128 devices: a whole 4x4x4 slice. The times are simulated.
128 devices in a mesh: shell: 4 (over z_lo, core), blk: 32 (over y, z_hi, x).
Axes of the slice: x: 4, y: 4, z: 4 (z_hi: 2, z_lo: 2; z = z_hi * 2 + z_lo), core: 2. Of those that a mesh axis runs over, the one named last changes fastest.
Arguments:
- plasma_state: float32 [8, 16384, 512], P(None, ('shell', 'blk')), may hold values from -6 to 6
- jacobian: float32 [3, 8, 8, 16384], P(None, None, None, ('shell', 'blk'))
- send_list: int32 [4, 286720], P(None, ('shell', 'blk')), may hold values from 0 to 127, as said below
- recv_map: int32 [262144], P(('shell', 'blk')), may hold values from 0 to 2240, as said below
- visit_point: int32 [524288], P(('shell', 'blk')), may hold values from 0 to 131072, as said below
- visit_cell: int32 [524288], P(('shell', 'blk')), may hold values from 0 to 65535, as said below
- conductance: float32 [1024, 512], P('shell'), may hold values from 1 to 1000
- lengths: int32 [1024], P('shell'), may hold values from 128 to 500, as said below
Outputs:
- new_state: float32 [8, 16384, 512], P(None, ('shell', 'blk'))
- thread_temp: float32 [1024, 512], P(('shell', 'blk'))
Inputs may be any that keep to these rules, and one draw needn't show every extreme that they name: `send_list`: row 0 is a source block of the sending device, row 1 the face opposite the receiving face, row 2 the level code (3: empty slot), row 3 the quadrant. Column s * 70 + c is slot c of what goes to the device of blk index s; some device fills all 70 slots to one peer in every draw. Level 0 stands only in slots c < 17; slots from 17 on hold levels 1, 2 or 3. `recv_map`: four entries per block and angular face, block-major then face. Each face takes one piece of level 0 or 1, or four pieces of level 2 with quadrants 0 to 3; exactly 128 faces of each device take four. Every used send slot is named exactly once. `visit_point`: t * 512 + i names point i of thread t of the device's shell group; the value 256 * 512 marks an unused slot. In a shell group every point below its thread's length is named exactly once, no other point is named. A device's slots form 8 aligned runs of 512 slots; the points named in one run belong to threads of one device (thread t to blk index t div 8), and the runs of one device name points of different devices. `visit_cell`: distinct cells of the device, block * 8^3 + cell. `lengths`: some thread of each shell group has 500 points.
All inputs are finite; a program needn't handle non-finite values. Where the computation divides by a largest or mean magnitude, that divisor is 1e-20 or more.
Results may differ from a plain program's by a relative error of at most 0.0003.
Values sent between devices are 32-bit elements; how exact they have to be, the bound alone decides.
A program may use at most 192 MiB of HBM per device.

v0:
```python
import jax
import jax.numpy as jnp
from jax import lax
from jax.sharding import PartitionSpec as P

BS = 8


CFL_NUMBER = 0.3
HIGH = lax.Precision.HIGHEST


def with_halo(array, sides, width):
    for axis, dim in sides:
        size, length = (lax.axis_size(axis), array.shape[dim])
        up = [(i, (i + 1) % size) for i in range(size - 1)]
        down = [(j, i) for i, j in up]
        last = lax.slice_in_dim(array, length - width, length, axis=dim)
        first = lax.slice_in_dim(array, 0, width, axis=dim)
        before = lax.ppermute(last, axis, up)
        after = lax.ppermute(first, axis, down)
        array = jnp.concatenate([before, array, after], axis=dim)
    return array


def face_select():
    square = BS * BS
    slot = jnp.arange(square, dtype=jnp.int32)
    outer = slot // BS
    inner = slot % BS
    cells_of = jnp.concatenate(
        [
            outer * square + inner,
            outer * square + (BS - 1) * BS + inner,
            outer * square + inner * BS,
            outer * square + inner * BS + BS - 1,
        ]
    )
    cell_ids = jnp.arange(BS * BS * BS, dtype=jnp.int32)
    return (cell_ids[:, None] == cells_of[None, :]).astype(jnp.float32)


def piece_tables():
    half_edge = BS // 2
    square = BS * BS
    source = jnp.arange(square, dtype=jnp.int32)
    target = jnp.arange(square, dtype=jnp.int32)
    src_row = (source // BS)[:, None]
    src_col = (source % BS)[:, None]
    dst_row = (target // BS)[None, :]
    dst_col = (target % BS)[None, :]
    dst_quad = dst_row // half_edge * 2 + dst_col // half_edge
    mats = [(src_row == dst_row) & (src_col == dst_col)]
    for quad in range(4):
        mats.append(
            (src_row == quad // 2 * half_edge + dst_row // 2)
            & (src_col == quad % 2 * half_edge + dst_col // 2)
        )
    full = [m.astype(jnp.float32) for m in mats]
    for quad in range(4):
        near = (
            (src_row // 2 == dst_row % half_edge)
            & (src_col // 2 == dst_col % half_edge)
            & (dst_quad == quad)
        )
        full.append(0.25 * near.astype(jnp.float32))
    return jnp.concatenate(full, axis=1)


def select_apply(rows, table, choice_index, options, width):
    product = jnp.einsum("fpc,cm->fpm", rows, table, precision=HIGH)
    fields, count = (rows.shape[0], rows.shape[1])
    weights = (choice_index[:, None] == jnp.arange(options, dtype=jnp.int32)[None, :]).astype(
        jnp.float32
    )
    product = product.reshape(fields, count, options, width)
    return jnp.sum(product * weights[None, :, :, None], axis=2)


def face_rows_of(face_flat, send_list):
    source_row = send_list[0] * 4 + send_list[1]
    return jnp.take(face_flat, source_row, axis=1)


def pack_pieces(face_flat, send_list):
    rows = face_rows_of(face_flat, send_list)
    level_code = send_list[2]
    quadrant = send_list[3]
    index = jnp.where(
        level_code == 0,
        0,
        jnp.where(level_code == 1, 1 + quadrant, jnp.where(level_code == 2, 5 + quadrant, -1)),
    )
    return select_apply(rows, piece_tables(), index, 9, BS * BS)


def assemble_ghosts(received, recv_map, blocks):
    fields, square = (received.shape[0], received.shape[2])
    padded_rows = jnp.concatenate([received, jnp.zeros((fields, 1, square), jnp.float32)], axis=1)
    taken = jnp.take(padded_rows, recv_map, axis=1).reshape(fields, blocks, 4, 4, square)
    return jnp.sum(taken, axis=3)


def advance(
    flat_state, ghosts, lower_rim, upper_rim, jacobian, wave_speed, step_ratio, select_table
):
    fields, blocks, cells = flat_state.shape
    square = BS * BS
    cell_ids = jnp.arange(cells, dtype=jnp.int32)[None, None, :]
    first_coord = cell_ids // BS % BS
    second_coord = cell_ids % BS

    def spread(face_index):
        table = select_table[:, face_index * square : (face_index + 1) * square]
        return jnp.einsum("fbk,ck->fbc", ghosts[:, :, face_index], table, precision=HIGH)

    def shift_pair(stride, coord, low_face, high_face):
        pad = jnp.zeros((fields, blocks, stride), jnp.float32)
        below = jnp.concatenate([pad, flat_state[:, :, : cells - stride]], axis=2)
        above = jnp.concatenate([flat_state[:, :, stride:], pad], axis=2)
        below = jnp.where(coord == 0, spread(low_face), below)
        above = jnp.where(coord == BS - 1, spread(high_face), above)
        return (below, above)

    radial_low = jnp.concatenate([lower_rim, flat_state[:, :, : cells - square]], axis=2)
    radial_high = jnp.concatenate([flat_state[:, :, square:], upper_rim], axis=2)
    neighbours = [
        (radial_low, radial_high),
        shift_pair(BS, first_coord, 0, 1),
        shift_pair(1, second_coord, 2, 3),
    ]
    change_sum = jnp.zeros_like(flat_state)
    for direction in range(3):
        below, above = neighbours[direction]
        averaged = jnp.einsum("ghb,hbc->gbc", jacobian[direction], above - below, precision=HIGH)
        spread_term = wave_speed[direction][None, :, None] * (above - 2.0 * flat_state + below)
        change_sum = change_sum + 0.5 * averaged - 0.5 * spread_term
    return flat_state - step_ratio * change_sum


def thread_solve(samples, conductance, lengths):
    points = samples.shape[1]
    position = jnp.arange(points, dtype=jnp.int32)[None, :]
    link_weight = jnp.where(
        position + 1 < lengths[:, None], conductance, jnp.zeros_like(conductance)
    )
    before = jnp.concatenate(
        [jnp.zeros((link_weight.shape[0], 1), jnp.float32), link_weight[:, :-1]], axis=1
    )
    diagonal = 1.0 + before + link_weight
    solved = lax.linalg.tridiagonal_solve(-before, diagonal, -link_weight, samples[:, :, None])
    return solved[:, :, 0]


def on_device(
    plasma_state, jacobian, send_list, recv_map, visit_point, visit_cell, conductance, lengths
):
    fields, blocks, cells = plasma_state.shape
    square = BS * BS
    wave_speed = jnp.max(jnp.sum(jnp.abs(jacobian), axis=2), axis=1)
    fastest = lax.pmax(jnp.max(wave_speed), ("shell", "blk"))
    step_ratio = CFL_NUMBER / fastest
    inner_rim = plasma_state[:, :, :square]
    outer_rim = plasma_state[:, :, cells - square :]
    radial_rims = jnp.stack([inner_rim, outer_rim], axis=0)
    widened = with_halo(radial_rims, (("shell", 0),), 1)
    shell_index = lax.axis_index("shell")
    lower_rim = jnp.where(shell_index == 0, inner_rim, widened[0])
    upper_rim = jnp.where(shell_index == lax.axis_size("shell") - 1, outer_rim, widened[3])
    select_table = face_select()
    face_flat = jnp.einsum("fbc,ck->fbk", plasma_state, select_table, precision=HIGH).reshape(
        fields, blocks * 4, square
    )
    peers = lax.axis_size("blk")
    slot_count = send_list.shape[1] // peers
    pieces = pack_pieces(face_flat, send_list)
    arrived = lax.all_to_all(
        pieces.reshape(fields, peers * slot_count * square),
        "blk",
        split_axis=1,
        concat_axis=1,
        tiled=True,
    )
    arrived = arrived.reshape(fields, peers * slot_count, square)
    ghosts = assemble_ghosts(arrived, recv_map, blocks)
    advanced = advance(
        plasma_state, ghosts, lower_rim, upper_rim, jacobian, wave_speed, step_ratio, select_table
    )
    pressure = advanced[fields - 1].reshape(-1)
    sampled = pressure[visit_cell]
    group_points = conductance.shape[0] * conductance.shape[1]
    visited = visit_point < group_points
    own_count = conductance.shape[0] // peers
    first_row = lax.axis_index("blk") * own_count
    own_kappa = lax.dynamic_slice_in_dim(conductance, first_row, own_count, 0)
    own_lengths = lax.dynamic_slice_in_dim(lengths, first_row, own_count, 0)
    contribution = jnp.zeros((group_points,), jnp.float32).at[visit_point].set(sampled, mode="drop")
    own_rows = lax.psum_scatter(contribution, "blk", scatter_dimension=0, tiled=True)
    thread_temp = thread_solve(own_rows.reshape(own_count, -1), own_kappa, own_lengths)
    all_values = lax.all_gather(thread_temp.reshape(-1), "blk", axis=0, tiled=True)
    extended = jnp.concatenate([all_values, jnp.zeros((1,), jnp.float32)])
    returned = extended[visit_point]
    updated = jnp.where(visited, returned, sampled)
    new_pressure = pressure.at[visit_cell].set(updated)
    new_state = advanced.at[fields - 1].set(new_pressure.reshape(blocks, cells))
    return (new_state, thread_temp)


def solution(mesh):
    in_specs = (
        P(None, ("shell", "blk"), None),
        P(None, None, None, ("shell", "blk")),
        P(None, ("shell", "blk")),
        P(("shell", "blk")),
        P(("shell", "blk")),
        P(("shell", "blk")),
        P("shell", None),
        P("shell"),
    )
    out_specs = (P(None, ("shell", "blk"), None), P(("shell", "blk"), None))
    return jax.shard_map(
        on_device, mesh=mesh, in_specs=in_specs, out_specs=out_specs, check_vma=False
    )
```

profile of v0, /device:TPU:0, one launch (start us, length us, event | category | flops | bytes accessed | tf_op | source)
XLA Modules:
  0.0 1025.7 jit_solution(2453170375769610498)
XLA Ops:
  7.4 2.9 convolution_bitcast_fusion
  10.6 1.7 reshape.1007
  12.2 2.8 copy.917
  15.3 7.8 gather_fusion
  23.1 14.0 %select_bitcast_fusion = f32[8,2240,64]{2,0,1:T(8,128)} fusion(f32[2240,8,64]{2,1,0:T(8,128)} %gather_fusion, pred[2240]{0:T(1024)(128)(4,1)S(1)} %compare_and_fusion.5), kind=kLoop, calls=%fused_computation.617 | loop fusion | flops 1146880 | bytes 9177280 | tf_op jit(solution)/shard_map/jit(_take)/select_n | solution.py:82
  37.4 41.6 %fusion.352 = f32[8,2240,576]{1,2,0:T(8,128)} fusion(f32[8,2240,64]{2,0,1:T(8,128)} %select_bitcast_fusion, f32[64,576]{1,0:T(8,128)S(1)} %concatenate.65), kind=kOutput, calls=%fused_computation.615 | convolution fusion | flops 7927234560 | bytes 46022656 | tf_op jit(solution)/shard_map/fpc,cm->fpm/dot_general | solution.py:71
  79.0 19.2 %multiply_reduce_fusion = f32[8,2240,64]{1,2,0:T(8,128)} fusion(f32[8,2240,9,64]{1,3,2,0:T(8,128)} %bitcast.3743, f32[2240,9]{0,1:T(8,128)S(1)} %fusion.385), kind=kLoop, calls=%fused_computation.614 | loop fusion | flops 19496960 | bytes 45955840 | tf_op jit(solution)/shard_map/reduce_sum | solution.py:77
  98.2 7.5 copy.919
  105.7 8.5 all_to_all.6
  114.2 7.1 copy.920
  121.3 10.8 %all-to-all-start = ((f32[8,32,4480]{2,0,1:T(8,128)}), f32[8,32,4480]{2,0,1:T(8,128)}, u32[]{:S(2)}, u32[]{:S(2)}) async-start(f32[8,32,4480]{2,0,1:T(8,128)} %copy.920), calls=%async_computation | async-start | bytes 9175040 | tf_op jit(solution)/shard_map/all_to_all | solution.py:177
  132.2 2.8 copy.937
  135.0 1.1 slice_bitcast_fusion.8
  136.2 1.3 collective-permute-start
  137.5 3.8 collective-permute-start.1
  141.4 0.6 fusion.548
  142.3 2.8 fusion.720
  145.1 2.7 fusion.719
  147.8 2.8 fusion.721
  150.6 99.7 %pmax.7 = f32[]{:T(128)} all-reduce(f32[]{:T(128)} %get-tuple-element.339), channel_id=1, replica_groups=mesh['shell'=4,'blk'=32] {'shell','blk'}, use_global_device_ids=true, to_apply=%region_2.0 | all-reduce | flops 1 | bytes 8 | tf_op jit(solution)/shard_map/pmax | solution.py:161
  250.6 1.0 copy.1060
  251.6 1.0 copy.1057
  252.6 1.0 copy.1063
  254.6 1.0 fusion.717
  255.5 0.8 copy-done.14
  256.3 1.4 bitcast_select_fusion.1
  257.8 5.2 fusion.371
  263.0 5.4 copy.921
  268.4 7.8 reshape.1009
  276.2 9.0 copy.922
  285.2 3.7 concatenate.66
  289.0 19.5 %gather_fusion.1 = f32[2048,8,64]{2,1,0:T(8,128)} fusion(f32[8,2241,64]{2,0,1:T(8,128)} %concatenate.66, s32[2048]{0:T(1024)S(1)} %fusion.395), kind=kCustom, calls=%fused_computation.1 | custom fusion | bytes 8396800 | tf_op jit(solution)/shard_map/jit(_take)/gather | solution.py:100
  308.4 7.3 select_reduce_fusion
  315.7 2.3 fusion.376
  318.1 2.3 fusion.375
  320.4 1.1 pad_select_fusion
  322.0 1.1 pad_select_fusion.1
  323.3 3.3 fusion.369
  326.7 12.9 %fusion.356 = f32[8,128,512]{2,0,1:T(8,128)} fusion(f32[8,128,512]{2,0,1:T(8,128)} %fusion.375, f32[8,128,511]{2,0,1:T(8,128)} %get-tuple-element.554, f32[8,128,512]{2,0,1:T(8,128)} %fusion.376, f32[8,128,511]{2,0,1:T(8,128)S(1)} %copy-done.3, f32[8,128,512]{2,0,1:T(8,128)} %copy-done.4, f32[8,128,512]{2,0,1:T(8,128)} %copy-done.5, ...), kind=kOutput, calls=%fused_computation.624 | convolution fusion | flops 66060288 | bytes 25192964 | tf_op jit(solution)/shard_map/ghb,hbc->gbc/dot_general | solution.py:135
  339.6 1.9 slice.2292
  341.5 23.0 %gather_fusion.2 = f32[4096]{0:T(1024)S(1)} fusion(f32[65536]{0:T(1024)S(1)} %bitcast.3740, s32[4096]{0:T(1024)S(1)} %get-tuple-element.565), kind=kCustom, calls=%fused_computation.2 | custom fusion | bytes 49152 | tf_op jit(solution)/shard_map/gather | solution.py:190
  364.5 16.3 %scatter_custom_fusion = f32[131072]{0:T(1024)} fusion(s32[4096]{0:T(1024)S(1)} %get-tuple-element.564, f32[4096]{0:T(1024)S(1)} %gather_fusion.2, f32[]{:T(128)} %constant.352.clone.1), kind=kCustom, calls=%fused_computation.667 | custom fusion | bytes 524292 | tf_op jit(solution)/shard_map/scatter | solution.py:197
  381.5 0.6 dynamic-slice.7
  382.6 345.7 %all-reduce.9.cloned.1.call-done = f32[131072]{0:T(1024)} async-done(((f32[131072]{0:T(1024)}), f32[131072]{0:T(1024)}) %all-reduce.9.cloned.1.call-update) | async-done | bytes 524304
  728.4 0.7 dynamic-slice.8
  729.3 0.5 slice_reduce_fusion
  730.3 90.9 %while.33 = (s32[]{:T(128)}, f32[8]{0:T(128)S(1)}, f32[8,1]{0,1:T(1,128)S(1)}, f32[15,32,8]{1,0,2:T(8,128)S(1)}, f32[15,32,8,1]{1,0,2,3:T(8,128)S(1)}, /*index=5...) while((s32[]{:T(128)}, f32[8]{0:T(128)S(1)}, ...), condition=%wide.region_9.10_spmd, body=%wide.region_8.9_spmd.sunk | while | flops 1585 | bytes 19529 | solution.py:151
  730.6 0.5 fusion.727
  736.6 0.5 fusion.727
  742.7 0.5 fusion.727
  748.7 0.5 fusion.727
  754.8 0.5 fusion.727
  760.8 0.5 fusion.727
  766.8 0.5 fusion.727
  772.9 0.5 fusion.727
  778.9 0.5 fusion.727
  785.0 0.5 fusion.727
  829.1 45.3 %while.34 = (s32[]{:T(128)}, f32[8,1]{0,1:T(1,128)S(1)}, f32[15,32,8,1]{1,0,2,3:T(8,128)S(1)}, f32[15,32,8,1]{2,3,1,0:T(1,128)S(1)}, f32[15,32,8]{2,1,0:T(8,128)...) while((s32[]{:T(128)}, f32[8,1]{0,1:T(1,128)S(1)}, ...), condition=%wide.region_11.12_spmd, body=%wide.region_10.11_spmd.sunk | while | flops 546 | bytes 10161 | solution.py:151
  877.4 0.7 fusion.391
  878.1 96.9 %all_gather.3 = f32[131072]{0:T(1024)S(1)} all-gather(f32[4096]{0:T(1024)S(1)} %bitcast.3760), channel_id=1, replica_groups=mesh['shell'=4,'blk'=32] {'blk'}, dimensions={0}, use_global_device_ids=true | all-gather | bytes 540672 | tf_op jit(solution)/shard_map/all_gather | solution.py:200
  975.1 23.0 %gather_fusion.3 = f32[4096]{0:T(1024)S(1)} fusion(f32[131073]{0:T(1024)S(1)} %pad_maximum_fusion.4, s32[4096]{0:T(1024)S(1)} %get-tuple-element.563), kind=kCustom, calls=%fused_computation.3 | custom fusion | bytes 49152 | tf_op jit(solution)/shard_map/gather | solution.py:202
  998.2 15.7 %scatter_fusion = f32[65536]{0:T(1024)S(1)} fusion(f32[65536]{0:T(1024)S(1)} %bitcast.3741, s32[4096]{0:T(1024)S(1)} %get-tuple-element.566, f32[4096]{0:T(1024)S(1)} %compare_select_fusion.10), kind=kCustom, calls=%fused_computation.5 | custom fusion | bytes 65536 | tf_op jit(solution)/shard_map/scatter | solution.py:204
  1013.9 2.2 scatter.21
  1016.1 2.5 copy.1039
  (1820 shorter events, 143.9 us)
Async XLA Ops:
  7.2 134.2 %copy-start = (f32[256,512]{1,0:T(8,128)S(1)}, f32[256,512]{1,0:T(8,128)}, u32[]{:S(2)}) copy-start(f32[256,512]{1,0:T(8,128)} %param.20) | copy-start | bytes 1572868
  12.2 2.8 copy-start.17
  121.3 141.7 %all-to-all-start = ((f32[8,32,4480]{2,0,1:T(8,128)}), f32[8,32,4480]{2,0,1:T(8,128)}, u32[]{:S(2)}, u32[]{:S(2)}) async-start(f32[8,32,4480]{2,0,1:T(8,128)} %copy.920), calls=%async_computation | async-start | bytes 9175040 | tf_op jit(solution)/shard_map/all_to_all | solution.py:177
  132.1 596.2 %all-reduce.9.cloned.1.call-start = ((), (), s32[]{:S(2)}) async-start(), calls=%async_computation.1 | async-start | bytes 1048576
  135.0 6.4 copy-start.15
  135.0 7.0 copy-start.18
  135.0 7.0 copy-start.19
  135.0 7.0 copy-start.16
  136.2 119.4 %collective-permute-start = (f32[1,8,128,64]{3,1,2,0:T(8,128)}, f32[1,8,128,64]{3,1,2,0:T(8,128)S(1)}, u32[]{:S(2)}, u32[]{:S(2)}) collective-permute-start(f32[1,8,128,64]{3,1,2,0:T(8,128)} %get-tuple-element.549), channel_id=1, source_target_pairs={{32,0},{64,32},{96,64},{33,1},{65,33},{97,65},{34,2},{66,34},{98,6... | collective-permute-start | bytes 786440 | tf_op jit(solution)/shard_map/ppermute | solution.py:21
  137.5 118.9 %collective-permute-start.1 = (f32[1,8,128,64]{3,1,2,0:T(8,128)}, f32[1,8,128,64]{3,1,2,0:T(8,128)}, u32[]{:S(2)}, u32[]{:S(2)}) collective-permute-start(f32[1,8,128,64]{3,1,2,0:T(8,128)} %get-tuple-element.550), channel_id=1, source_target_pairs={{0,32},{32,64},{64,96},{1,33},{33,65},{65,97},{2,34},{34,66},{66,9... | collective-permute-start | bytes 786440 | tf_op jit(solution)/shard_map/ppermute | solution.py:20
  147.8 106.0 %copy-start.20 = (s32[256]{0:T(256)S(1)}, s32[256]{0:T(256)}, u32[]{:S(2)}) copy-start(s32[256]{0:T(256)} %param.21) | copy-start | bytes 3076
  254.6 3.2 copy-start.6
  255.5 0.8 copy-start.14
  315.7 4.7 copy-start.9
  320.4 1.6 copy-start.8
  321.5 1.5 copy-start.4
  322.0 1.3 copy-start.12
  323.3 3.3 copy-start.5
  323.3 3.3 copy-start.2
  323.3 3.3 copy-start.3
  323.3 3.5 copy-start.11
  341.5 39.4 %copy-start.10 = (f32[8,512]{0,1:T(8,128)S(1)}, f32[8,512]{0,1:T(8,128)}, u32[]{:S(2)}) copy-start(f32[8,512]{0,1:T(8,128)} %get-tuple-element.542) | copy-start | bytes 49156
  364.5 16.5 %copy-start.13 = (f32[8,512]{0,1:T(8,128)S(1)}, f32[8,512]{0,1:T(8,128)}, u32[]{:S(2)}) copy-start(f32[8,512]{0,1:T(8,128)} %get-tuple-element.541) | copy-start | bytes 49156
  380.8 0.7 copy-start.21
  998.2 15.7 %copy-start.7 = (f32[8,128,512]{2,0,1:T(8,128)S(1)}, f32[8,128,512]{2,0,1:T(8,128)}, u32[]{:S(2)}) copy-start(f32[8,128,512]{2,0,1:T(8,128)} %fusion.356) | copy-start | bytes 6291460
  1013.8 4.8 copy-start.1
Sparse Core Ops, SparseCore 0:
  381.0 347.3 all-reduce.8
where the time goes:
time: 1030 us
  waiting for transfers between devices  346 us (34%)
  local copies, waits for them, and re-layouts  320 us (31%)
  blocking collectives  197 us (19%)
  matrix products  72.7 us (7%)
  other arithmetic  56.5 us (5%)
  between operations  16.3 us (2%)
  starting transfers between devices  16 us (2%)
    unnamed x2, waiting for transfers between devices  346 us
    broadcast_in_dim x1534, local copies, waits for them, and re-layouts, thread_solve(): lax.linalg.tridiagonal_solve(-before, diagonal, -link_weight, samples[:,...  124 us
    pmax x1, blocking collectives, on_device(): fastest = lax.pmax(jnp.max(wave_speed), ('shell', 'blk'))  99.7 us
    all_gather x1, blocking collectives, on_device(): lax.all_gather(thread_temp.reshape(-1), 'blk', axis=0, tiled=True)  96.9 us
    dot_general x1, matrix products, select_apply(): product = jnp.einsum('fpc,cm->fpm', rows, table, precision=HIGH)  41.6 us
    gather x1, local copies, waits for them, and re-layouts, on_device(): sampled = pressure[visit_cell]  23 us
    gather x1, local copies, waits for them, and re-layouts, on_device(): returned = extended[visit_point]  23 us
    dot_general x3, matrix products, advance(): jnp.einsum('ghb,hbc->gbc', jacobian[direction], above - below, precision=...  21.4 us
  transfers between devices with their start and end apart: 4, of which 1 were waited for; matrix products, arithmetic and copies ran while one was open for 2% of the time, Pallas kernels for 0%

commit v1 on v0

v1 whole, which is shorter than its diff:
```python
import functools

import jax
import jax.numpy as jnp
from jax import lax
from jax.experimental import pallas as pl
from jax.experimental.pallas import tpu as pltpu
from jax.sharding import PartitionSpec as P

BS = 8
FULL = 17
CFL_NUMBER = 0.3
MESH = pl.DeviceIdType.MESH
F32 = jnp.float32
BF16 = jnp.bfloat16
VMEM_BYTES = 56 * 1024 * 1024


def params(collective=None):
    if collective is None:
        return pltpu.CompilerParams(vmem_limit_bytes=VMEM_BYTES)
    return pltpu.CompilerParams(
        vmem_limit_bytes=VMEM_BYTES, collective_id=collective, has_side_effects=True
    )


def iota(shape, dim):
    return lax.broadcasted_iota(jnp.int32, shape, dim)


def one_hot(mask):
    return jnp.where(mask, 1.0, 0.0).astype(BF16)


def high_low(x):
    high = x.astype(BF16).astype(F32)
    return high, x - high


def half_roll(x):
    shape = x.shape
    return pltpu.roll(x.reshape(-1, 8, 128), 4, 1).reshape(shape)


def pack_kernel(state, jac, cidx, copt, ccode, vp, u_out, slabs, ws, wmax, table, mean):
    fields = state.shape[0]
    for f in range(fields):
        u_out[f] = state[f].T.reshape(8, 64, 128)
    speed = jnp.max(jnp.sum(jnp.abs(jac[...]), axis=2), axis=1)
    ws[...] = speed
    wmax[...] = jnp.broadcast_to(jnp.max(speed), (8, 128))
    low_half = iota((1, 1, 1, 8, 128), 3) < 4
    for j in range(4):
        if j == 0:
            face = u_out[:, :, 0:8, :]
        elif j == 1:
            face = u_out[:, :, 56:64, :]
        else:
            face = u_out[:, :, pl.ds(0 if j == 2 else 7, 8, stride=8), :]
        parts = face.reshape(8, 2, 2, 2, 8, 128)
        first, second = parts[:, :, :, 0], parts[:, :, :, 1]
        left = jnp.where(low_half, first, half_roll(second))
        right = jnp.where(low_half, half_roll(first), second)
        lanes = slice(j * 128, (j + 1) * 128)
        pairs = face.reshape(8, 4, 2, 8, 128)
        mean[...] = (pairs[:, :, 0] + pairs[:, :, 1]).reshape(256, 128)
        rest = 0.25 * (mean[pl.ds(0, 128, stride=2), :] + mean[pl.ds(1, 128, stride=2), :])
        options = [
            left[:, 0].reshape(128, 128),
            right[:, 0].reshape(128, 128),
            left[:, 1].reshape(128, 128),
            right[:, 1].reshape(128, 128),
            rest,
        ]
        for option, rows in enumerate(options):
            high, low = high_low(rows)
            table[option * 128 : (option + 1) * 128, lanes] = high.astype(BF16)
            table[640 + option * 128 : 768 + option * 128, lanes] = low.astype(BF16)

    points = vp[...]
    used = points < 256 * 512
    owner = jnp.max(jnp.where(used, points >> 12, -1), axis=1, keepdims=True)
    local = jnp.where(used, points & 4095, -1).astype(F32) + 1.0

    def pair(i, carry):
        index = cidx[pl.ds(i, 1), :]
        option = copt[pl.ds(i, 1), :]
        codes = ccode[pl.ds(i, 1), :]
        picks = one_hot(iota((512, 256), 0) == index)
        got = jnp.dot(table[...], picks, preferred_element_type=F32)
        chosen = got[0:128] + got[640:768]
        for o in range(1, 5):
            chosen = jnp.where(
                option == o, got[o * 128 : (o + 1) * 128] + got[640 + o * 128 : 768 + o * 128], chosen
            )
        for half in range(2):
            peer = 2 * i + half
            lanes = slice(half * 128, half * 128 + 128)
            slabs[peer, 0:128, :] = chosen[:, lanes]
            run = jnp.sum(jnp.where(owner == peer, local, 0.0), axis=0, keepdims=True) - 1.0
            rows = [codes[:, lanes]] + [run[:, c * 128 : (c + 1) * 128] for c in range(4)]
            rows += [jnp.zeros((3, 128), F32)]
            slabs[peer, 128:136, :] = jnp.concatenate(rows, axis=0)
        return carry

    lax.fori_loop(0, 16, pair, 0)


def exchange_kernel(
    peers, shells, slabs, u, wmax, recv, lower, upper, gmax,
    send_sem, recv_sem, rim_send, rim_recv, own_sem, shell_max, group_max, blk_max,
    ssend, srecv, bsend, brecv,
):
    me = lax.axis_index("blk")
    shell = lax.axis_index("shell")
    barrier = pltpu.get_barrier_semaphore()

    def greet(d, carry):
        pl.semaphore_signal(
            barrier, inc=1, device_id={"blk": lax.rem(me + d, peers)}, device_id_type=MESH
        )
        return carry

    lax.fori_loop(1, peers, greet, 0)
    for d in range(1, shells):
        pl.semaphore_signal(
            barrier, inc=1, device_id={"shell": lax.rem(shell + d, shells)}, device_id_type=MESH
        )
    pl.semaphore_wait(barrier, peers + shells - 2)

    def shell_copy(d):
        return pltpu.make_async_remote_copy(
            src_ref=wmax, dst_ref=shell_max.at[d], send_sem=ssend.at[d], recv_sem=srecv.at[d],
            device_id={"shell": lax.rem(shell + d, shells)}, device_id_type=MESH,
        )

    for d in range(1, shells):
        shell_copy(d).start()

    def slab_copy(d):
        return pltpu.make_async_remote_copy(
            src_ref=slabs.at[lax.rem(me + d, peers)], dst_ref=recv.at[me],
            send_sem=send_sem.at[d], recv_sem=recv_sem.at[d],
            device_id={"blk": lax.rem(me + d, peers)}, device_id_type=MESH,
        )

    def start_slab(d, carry):
        slab_copy(d).start()
        return carry

    lax.fori_loop(1, peers, start_slab, 0)
    own = pltpu.make_async_copy(slabs.at[me], recv.at[me], own_sem.at[0])
    own.start()

    def rim_up():
        return pltpu.make_async_remote_copy(
            src_ref=u.at[:, 7], dst_ref=lower, send_sem=rim_send.at[0], recv_sem=rim_recv.at[0],
            device_id={"shell": lax.rem(shell + 1, shells)}, device_id_type=MESH,
        )

    def rim_down():
        return pltpu.make_async_remote_copy(
            src_ref=u.at[:, 0], dst_ref=upper, send_sem=rim_send.at[1], recv_sem=rim_recv.at[1],
            device_id={"shell": lax.rem(shell + shells - 1, shells)}, device_id_type=MESH,
        )

    own_lower = pltpu.make_async_copy(u.at[:, 0], lower, own_sem.at[1])
    own_upper = pltpu.make_async_copy(u.at[:, 7], upper, own_sem.at[2])

    @pl.when(shell < shells - 1)
    def _():
        rim_up().start()

    @pl.when(shell > 0)
    def _():
        rim_down().start()

    @pl.when(shell == 0)
    def _():
        own_lower.start()
        own_lower.wait()

    @pl.when(shell == shells - 1)
    def _():
        own_upper.start()
        own_upper.wait()

    best = wmax[...]
    for d in range(1, shells):
        shell_copy(d).wait()
        best = jnp.maximum(best, shell_max[d])
    group_max[...] = best

    def blk_copy(d):
        return pltpu.make_async_remote_copy(
            src_ref=group_max, dst_ref=blk_max.at[d], send_sem=bsend.at[d], recv_sem=brecv.at[d],
            device_id={"blk": lax.rem(me + d, peers)}, device_id_type=MESH,
        )

    def start_blk(d, carry):
        blk_copy(d).start()
        return carry

    lax.fori_loop(1, peers, start_blk, 0)

    def wait_blk(d, value):
        blk_copy(d).wait()
        return jnp.maximum(value, blk_max[d])

    gmax[...] = lax.fori_loop(1, peers, wait_blk, best)

    def wait_slab(d, carry):
        landing = pltpu.make_async_remote_copy(
            src_ref=slabs.at[lax.rem(me + d, peers)], dst_ref=recv.at[lax.rem(me + peers - d, peers)],
            send_sem=send_sem.at[d], recv_sem=recv_sem.at[d],
            device_id={"blk": lax.rem(me + d, peers)}, device_id_type=MESH,
        )
        landing.wait()
        return carry

    lax.fori_loop(1, peers, wait_slab, 0)
    own.wait()

    @pl.when(shell < shells - 1)
    def _():
        rim_up().wait_send()

    @pl.when(shell > 0)
    def _():
        rim_up().wait_recv()
        rim_down().wait_send()

    @pl.when(shell < shells - 1)
    def _():
        rim_down().wait_recv()


def assemble(recv, tgt, acc, ghosts, spread):
    def four(i, carry):
        tiles = []
        for s in range(4):
            slab = recv[4 * i + s]
            high, low = high_low(slab[0:128])
            tiles.append(
                jnp.concatenate([low, high, slab[128:136], jnp.zeros((8, 128), F32)], axis=0).astype(BF16)
            )
        rows = jnp.concatenate(tiles, axis=1)
        for n in range(4):
            lanes = slice(n * 512, (n + 1) * 512)
            picks = one_hot(iota((512, 512), 0) + i * 512 == tgt[:, lanes])
            part = jnp.dot(rows, picks, preferred_element_type=F32)
            acc[:, lanes] = jnp.where(i == 0, part, acc[:, lanes] + part)
        return carry

    acc[...] = jnp.zeros_like(acc)
    lax.fori_loop(0, recv.shape[0] // 4, four, 0)
    low_half = iota((1, 1, 8, 128), 2) < 4
    for j in range(4):
        values, codes = [], []
        for e in range(4):
            lanes = slice((j * 4 + e) * 128, (j * 4 + e + 1) * 128)
            values.append(acc[0:128, lanes] + acc[128:256, lanes])
            codes.append(acc[256:257, lanes])
        whole = codes[0] == 16.0
        coarse = (codes[0] == 32.0).reshape(1, 1, 1, 128)
        spread[pl.ds(0, 128, stride=2), :] = values[0]
        spread[pl.ds(1, 128, stride=2), :] = values[0]
        for i in range(2):
            quads = []
            for q in (2 * i, 2 * i + 1):
                fine = jnp.zeros((128, 128), F32)
                for e in range(4):
                    fine = jnp.where(codes[e] == 1.0 + q, values[e], fine)
                quads.append(jnp.where(whole, values[q], fine).reshape(8, 2, 8, 128))
            left, right = quads
            first = jnp.where(low_half, left, half_roll(right))
            second = jnp.where(low_half, half_roll(left), right)
            repeated = spread[...].reshape(8, 4, 8, 128)[:, 2 * i : 2 * i + 2]
            first = jnp.where(coarse, repeated, first)
            second = jnp.where(coarse, repeated, second)
            for xp in range(2):
                ghosts[j, :, 4 * i + 2 * xp] = first[:, xp]
                ghosts[j, :, 4 * i + 2 * xp + 1] = second[:, xp]


def step_cells(u, lower, upper, ghosts, jac, ws, ratio, padded, advanced):
    padded[:, 1:9, 8:72, :] = u[...]
    padded[:, 0, 8:72, :] = lower[...]
    padded[:, 9, 8:72, :] = upper[...]
    padded[:, 1:9, 0:8, :] = ghosts[0]
    padded[:, 1:9, 72:80, :] = ghosts[1]
    inner = iota((2, 8, 128), 1)

    def cell(n, carry):
        r, pair = n // 4, lax.rem(n, 4)
        a = pair * 2
        own = [padded[h, r + 1, pl.ds(pl.multiple_of(a * 8 + 8, 8), 16), :].reshape(2, 8, 128) for h in range(8)]
        total = [jnp.zeros((2, 8, 128), F32) for _ in range(8)]
        for d in range(3):
            gap = []
            speed = ws[d : d + 1, :].reshape(1, 1, 128)
            for h in range(8):
                if d == 0:
                    rows = pl.ds(pl.multiple_of(a * 8 + 8, 8), 16)
                    below = padded[h, r, rows, :].reshape(2, 8, 128)
                    above = padded[h, r + 2, rows, :].reshape(2, 8, 128)
                elif d == 1:
                    below = padded[h, r + 1, pl.ds(pl.multiple_of(a * 8, 8), 16), :].reshape(2, 8, 128)
                    above = padded[h, r + 1, pl.ds(pl.multiple_of(a * 8 + 16, 8), 16), :].reshape(2, 8, 128)
                else:
                    lows = [ghosts[2, h, r, pl.ds(a + k, 1), :] for k in range(2)]
                    highs = [ghosts[3, h, r, pl.ds(a + k, 1), :] for k in range(2)]
                    lows = jnp.stack([jnp.broadcast_to(x, (8, 128)) for x in lows])
                    highs = jnp.stack([jnp.broadcast_to(x, (8, 128)) for x in highs])
                    below = jnp.where(inner == 0, lows, pltpu.roll(own[h], 1, 1))
                    above = jnp.where(inner == 7, highs, pltpu.roll(own[h], 7, 1))
                gap.append(above - below)
                total[h] = total[h] - speed * (above - 2.0 * own[h] + below)
            for g in range(8):
                for h in range(8):
                    total[g] = total[g] + jac[d, g, h : h + 1, :].reshape(1, 1, 128) * gap[h]
        for g in range(8):
            advanced[g, r, pl.ds(pl.multiple_of(a * 8, 8), 16), :] = (
                own[g] - ratio * total[g]
            ).reshape(16, 128)
        return carry

    lax.fori_loop(0, 32, cell, 0)


def sample_points(pressure, vc, samples):
    high, low = high_low(pressure)
    rows = jnp.concatenate([high, low], axis=0).astype(BF16)

    def run(i, carry):
        where_to = vc[pl.ds(i, 1), :]
        picks = one_hot(iota((512, 512), 0) == (where_to & 511))
        got = jnp.dot(rows, picks, preferred_element_type=F32)
        got = got[0:128] + got[128:256]
        block = where_to >> 9
        samples[pl.ds(i, 1), :] = jnp.sum(
            jnp.where(iota((128, 512), 0) == block, got, 0.0), axis=0, keepdims=True
        )
        return carry

    lax.fori_loop(0, 8, run, 0)


def step_kernel(
    recv, tgt, u, lower, upper, gmax, jac, ws, vc, vp,
    new_state, samples, outgoing, tidx, acc, ghosts, spread, padded, advanced,
):
    assemble(recv, tgt, acc, ghosts, spread)
    ratio = 0.5 * (CFL_NUMBER / gmax[0:1, :]).reshape(1, 1, 128)
    step_cells(u, lower, upper, ghosts, jac, ws, ratio, padded, advanced)
    for f in range(8):
        new_state[f] = advanced[f].reshape(512, 128).T
    sample_points(new_state[7], vc, samples)
    tidx[...] = recv[:, 128:136, :]
    points = vp[...]
    owner = jnp.max(jnp.where(points < 256 * 512, points >> 12, -1), axis=1, keepdims=True)
    values = samples[...]
    peer = iota((32, 512), 0)
    total = jnp.zeros((32, 512), F32)
    for run in range(8):
        total = jnp.where(peer == owner[run : run + 1, :], values[run : run + 1, :], total)
    outgoing[...] = jnp.zeros_like(outgoing)
    for c in range(4):
        outgoing[:, c, :] = total[:, c * 128 : (c + 1) * 128]


def reduce_threads(weight, rhs):
    left, right = pltpu.roll(weight, 1, 1), weight
    excess = jnp.ones_like(weight)
    points = weight.shape[1]
    stride = 1
    while stride < points:
        inv = 1.0 / (excess + left + right)
        e, r = excess * inv, rhs * inv
        back, ahead = stride, points - stride
        new_excess = excess + left * pltpu.roll(e, back, 1) + right * pltpu.roll(e, ahead, 1)
        rhs = rhs + left * pltpu.roll(r, back, 1) + right * pltpu.roll(r, ahead, 1)
        left, right = (
            left * pltpu.roll(left * inv, back, 1),
            right * pltpu.roll(right * inv, ahead, 1),
        )
        excess = new_excess
        stride *= 2
    return rhs / (excess + left + right)


def thread_kernel(
    peers, outgoing, tidx, conductance, lengths, thread_temp, returned,
    arrived, picks, rows_of, back, own_sem, send_sem, recv_sem, bsend, brecv,
):
    me = lax.axis_index("blk")
    barrier = pltpu.get_barrier_semaphore()

    def greet(d, carry):
        pl.semaphore_signal(
            barrier, inc=1, device_id={"blk": lax.rem(me + d, peers)}, device_id_type=MESH
        )
        return carry

    lax.fori_loop(1, peers, greet, 0)
    pl.semaphore_wait(barrier, peers - 1)

    def copy(src, dst, slot, ssem, rsem, d):
        peer = lax.rem(me + d, peers)
        return pltpu.make_async_remote_copy(
            src_ref=src.at[peer], dst_ref=dst.at[slot], send_sem=ssem.at[d], recv_sem=rsem.at[d],
            device_id={"blk": peer}, device_id_type=MESH,
        )

    def start(d, carry):
        copy(outgoing, arrived, me, send_sem, recv_sem, d).start()
        return carry

    lax.fori_loop(1, peers, start, 0)
    own = pltpu.make_async_copy(outgoing.at[me], arrived.at[me], own_sem.at[0])
    own.start()

    def prepare(s, carry):
        point = jnp.concatenate([tidx[s, 1 + c : 2 + c, :] for c in range(4)], axis=1).astype(jnp.int32)
        picks[s] = one_hot(iota((128, 512), 0) == (point & 127))
        row = ((point >> 7) & 3) * 8 + (point >> 9)
        rows_of[s] = jnp.broadcast_to(jnp.where(point < 0, -1, row), (8, 512))
        return carry

    lax.fori_loop(0, peers, prepare, 0)
    own.wait()

    def gather(d, total):
        s = lax.rem(me + peers - d, peers)

        @pl.when(d > 0)
        def _():
            copy(outgoing, arrived, s, send_sem, recv_sem, d).wait()

        value = jnp.concatenate([arrived[s, c : c + 1, :] for c in range(4)], axis=1)
        high, low = high_low(value)
        mask = iota((32, 512), 0) == rows_of[s, 0:1, :]
        rows = jnp.concatenate([jnp.where(mask, high, 0.0), jnp.where(mask, low, 0.0)], axis=0)
        part = lax.dot_general(
            rows.astype(BF16), picks[s], (((1,), (1,)), ((), ())), preferred_element_type=F32
        )
        return total + part

    total = lax.fori_loop(0, peers, gather, jnp.zeros((64, 128), F32))
    total = total[0:32] + total[32:64]
    rhs = jnp.concatenate([total[c * 8 : (c + 1) * 8] for c in range(4)], axis=1)
    mine = pl.ds(pl.multiple_of(me * 8, 8), 8)
    weight = jnp.where(iota((8, 512), 1) + 1 < lengths[mine, :], conductance[mine, :], 0.0)
    solved = reduce_threads(weight, rhs)
    thread_temp[...] = solved
    high, low = high_low(solved)
    table = jnp.concatenate(
        [part[:, c * 128 : (c + 1) * 128] for part in (high, low) for c in range(4)], axis=0
    ).astype(BF16)

    def answer(d, carry):
        s = lax.rem(me + d, peers)
        got = jnp.dot(table, picks[s], preferred_element_type=F32)
        got = got[0:32] + got[32:64]
        mask = iota((32, 512), 0) == rows_of[s, 0:1, :]
        line = jnp.sum(jnp.where(mask, got, 0.0), axis=0, keepdims=True)
        back[s] = jnp.concatenate(
            [line[:, c * 128 : (c + 1) * 128] for c in range(4)] + [jnp.zeros((4, 128), F32)], axis=0
        )

        @pl.when(d > 0)
        def _():
            copy(back, returned, me, bsend, brecv, d).start()

        return carry

    lax.fori_loop(0, peers, answer, 0)
    mine_back = pltpu.make_async_copy(back.at[me], returned.at[me], own_sem.at[1])
    mine_back.start()

    def finish(d, carry):
        copy(back, returned, lax.rem(me + peers - d, peers), bsend, brecv, d).wait()
        return carry

    lax.fori_loop(1, peers, finish, 0)
    mine_back.wait()


def write_kernel(old, returned, vc, vp, new):
    points = vp[...]
    used = points < 256 * 512
    owner = jnp.max(jnp.where(used, points >> 12, -1), axis=1, keepdims=True)
    values = jnp.zeros((8, 512), F32)
    for o in range(returned.shape[0]):
        line = jnp.concatenate([returned[o, c : c + 1, :] for c in range(4)], axis=1)
        values = jnp.where(owner == o, line, values)
    where_to = vc[...]
    high, low = high_low(values)
    total = jnp.zeros((384, 512), F32)
    for run in range(8):
        picks = one_hot(iota((512, 512), 0) == (where_to[run : run + 1, :] & 511))
        block = jnp.where(used, where_to >> 9, -1)[run : run + 1, :]
        mask = iota((128, 512), 0) == block
        rows = jnp.concatenate(
            [
                jnp.where(mask, high[run : run + 1, :], 0.0),
                jnp.where(mask, low[run : run + 1, :], 0.0),
                jnp.where(mask, 1.0, 0.0),
            ],
            axis=0,
        ).astype(BF16)
        total = total + lax.dot_general(
            rows, picks, (((1,), (1,)), ((), ())), preferred_element_type=F32
        )
    new[0] = jnp.where(total[256:384] > 0.5, total[0:128] + total[128:256], old[0])


def column_plan(send_list, peers):
    send = send_list.reshape(4, peers, -1)
    block, face, level, quad = send[0], send[1], send[2], send[3]
    row = jnp.where(level == 3, -1, face * 128 + block)
    option = jnp.where(level == 1, quad, jnp.where(level == 2, 4, 0))
    code = jnp.where(level == 0, 16, jnp.where(level == 1, 32, jnp.where(level == 2, 1 + quad, 0)))
    spare = jnp.full((peers, 128 - row.shape[1] - 3 * FULL), -1, jnp.int32)
    head = row[:, :FULL]
    flat = jnp.zeros_like(head)
    cidx = jnp.concatenate([row, head, head, head, spare], axis=1)
    copt = jnp.concatenate([option, flat + 1, flat + 2, flat + 3, spare], axis=1)
    ccode = jnp.concatenate([code, flat, flat, flat, spare * 0], axis=1).astype(F32)
    half = peers // 2
    return cidx.reshape(half, 256), copt.reshape(half, 256), ccode.reshape(half, 256)


def targets(recv_map, peers, cap):
    named = recv_map.reshape(-1, 4, 4).transpose(1, 2, 0)
    valid = named < peers * cap
    sender, slot = named // cap, named % cap
    column = jnp.where(valid, sender * 128 + slot, -1)
    single = jnp.sum(valid.astype(jnp.int32), axis=1, keepdims=True) == 1
    lone = jnp.max(column, axis=1, keepdims=True)
    entry = jnp.arange(4, dtype=jnp.int32)[None, :, None]
    extra = jnp.where((lone & 127) < FULL, lone + cap + FULL * (entry - 1), -1)
    column = jnp.where(single, jnp.where(entry == 0, lone, extra), column)
    return column.reshape(1, -1)


def on_device(
    plasma_state, jacobian, send_list, recv_map, visit_point, visit_cell, conductance, lengths
):
    fields, blocks, cells = plasma_state.shape
    peers, shells = lax.axis_size("blk"), lax.axis_size("shell")
    cap = send_list.shape[1] // peers
    cidx, copt, ccode = column_plan(send_list, peers)
    tgt = targets(recv_map, peers, cap)
    vp = visit_point.reshape(8, -1)
    vc = visit_cell.reshape(8, -1)
    shape = jax.ShapeDtypeStruct
    u, slabs, ws, wmax = pl.pallas_call(
        pack_kernel,
        out_shape=[
            shape((fields, 8, 64, blocks), F32),
            shape((peers, 136, 128), F32),
            shape((3, blocks), F32),
            shape((8, 128), F32),
        ],
        scratch_shapes=[pltpu.VMEM((1280, 512), BF16), pltpu.VMEM((256, 128), F32)],
        compiler_params=params(),
        name="pack",
    )(plasma_state, jacobian, cidx, copt, ccode, vp)

    vmem = pl.BlockSpec(memory_space=pltpu.VMEM)
    recv, lower, upper, gmax = pl.pallas_call(
        functools.partial(exchange_kernel, peers, shells),
        in_specs=[vmem] * 3,
        out_specs=[vmem] * 4,
        out_shape=[
            shape((peers, 136, 128), F32),
            shape((fields, 64, blocks), F32),
            shape((fields, 64, blocks), F32),
            shape((8, 128), F32),
        ],
        scratch_shapes=[
            pltpu.SemaphoreType.DMA((peers,)),
            pltpu.SemaphoreType.DMA((peers,)),
            pltpu.SemaphoreType.DMA((2,)),
            pltpu.SemaphoreType.DMA((2,)),
            pltpu.SemaphoreType.DMA((3,)),
            pltpu.VMEM((shells, 8, 128), F32),
            pltpu.VMEM((8, 128), F32),
            pltpu.VMEM((peers, 8, 128), F32),
            pltpu.SemaphoreType.DMA((shells,)),
            pltpu.SemaphoreType.DMA((shells,)),
            pltpu.SemaphoreType.DMA((peers,)),
            pltpu.SemaphoreType.DMA((peers,)),
        ],
        compiler_params=params(1),
        name="exchange",
    )(slabs, u, wmax)

    stepped, samples, outgoing, tidx = pl.pallas_call(
        step_kernel,
        out_shape=[
            shape((fields, blocks, cells), F32),
            shape((8, 512), F32),
            shape((peers, 8, 128), F32),
            shape((peers, 8, 128), F32),
        ],
        scratch_shapes=[
            pltpu.VMEM((272, 2048), F32),
            pltpu.VMEM((4, fields, 8, 8, 128), F32),
            pltpu.VMEM((256, 128), F32),
            pltpu.VMEM((fields, 10, 80, 128), F32),
            pltpu.VMEM((fields, 8, 64, 128), F32),
        ],
        compiler_params=params(),
        name="step",
    )(recv, tgt, u, lower, upper, gmax, jacobian, ws, vc, vp)

    thread_temp, returned = pl.pallas_call(
        functools.partial(thread_kernel, peers),
        in_specs=[vmem] * 4,
        out_specs=[vmem] * 2,
        out_shape=[shape((8, 512), F32), shape((peers, 8, 128), F32)],
        scratch_shapes=[
            pltpu.VMEM((peers, 8, 128), F32),
            pltpu.VMEM((peers, 128, 512), BF16),
            pltpu.VMEM((peers, 8, 512), jnp.int32),
            pltpu.VMEM((peers, 8, 128), F32),
            pltpu.SemaphoreType.DMA((2,)),
            pltpu.SemaphoreType.DMA((peers,)),
            pltpu.SemaphoreType.DMA((peers,)),
            pltpu.SemaphoreType.DMA((peers,)),
            pltpu.SemaphoreType.DMA((peers,)),
        ],
        compiler_params=params(2),
        name="threads",
    )(outgoing, tidx, conductance, lengths.reshape(-1, 1))

    plane = pl.BlockSpec((1, blocks, cells), lambda i: (fields - 1, 0, 0))
    whole = lambda shape: pl.BlockSpec(shape, lambda i: (0,) * len(shape))
    new_state = pl.pallas_call(
        write_kernel,
        grid=(1,),
        in_specs=[plane, whole((peers, 8, 128)), whole((8, 512)), whole((8, 512))],
        out_specs=plane,
        out_shape=shape((fields, blocks, cells), F32),
        input_output_aliases={0: 0},
        compiler_params=params(),
        name="write",
    )(stepped, returned, vc, vp)
    return (new_state, thread_temp)


def solution(mesh):
    in_specs = (
        P(None, ("shell", "blk"), None),
        P(None, None, None, ("shell", "blk")),
        P(None, ("shell", "blk")),
        P(("shell", "blk")),
        P(("shell", "blk")),
        P(("shell", "blk")),
        P("shell", None),
        P("shell"),
    )
    out_specs = (P(None, ("shell", "blk"), None), P(("shell", "blk"), None))
    return jax.shard_map(
        on_device, mesh=mesh, in_specs=in_specs, out_specs=out_specs, check_vma=False
    )
```

time: 1030 us -> 128 us (0.12)
  waiting for transfers between devices: 346 us -> 0 us
  local copies, waits for them, and re-layouts: 320 us -> 8.06 us
  blocking collectives: 197 us -> 0 us
  Pallas kernels: 0 us -> 111 us
  matrix products: 72.7 us -> 0 us
  other arithmetic: 56.5 us -> 7.06 us
  starting transfers between devices: 16 us -> 0 us
  between operations: 16.3 us -> 0.82 us
    unnamed x2 -> x0, waiting for transfers between devices: 346 us -> none
    broadcast_in_dim x1535 -> x1, local copies, waits for them, and re-layouts: 124 us -> 0.01 us  [column_plan(): spare = jnp.full((peers, 128 - row.shape[1] - 3 * FULL), -1, jnp.int32)]
    pallas_call x0 -> x5, Pallas kernels: none -> 111 us  [the longest x1 48.2 us: on_device(): pl.pallas_call(functools.partial(exchange_kernel, peers, shells), in_spec...]
    pmax x1 -> x0, blocking collectives: 99.7 us -> none  [on_device(): fastest = lax.pmax(jnp.max(wave_speed), ('shell', 'blk'))]
    all_gather x1 -> x0, blocking collectives: 96.9 us -> none  [on_device(): lax.all_gather(thread_temp.reshape(-1), 'blk', axis=0, tiled=True)]
    gather x4 -> x0, local copies, waits for them, and re-layouts: 73.3 us -> none  [the longest x1 23 us: on_device(): sampled = pressure[visit_cell]]
    dot_general x9 -> x0, matrix products: 72.7 us -> none  [the longest x1 41.6 us: select_apply(): product = jnp.einsum('fpc,cm->fpm', rows, table, precision=HIGH)]
    scatter x3 -> x0, local copies, waits for them, and re-layouts: 34.2 us -> none  [the longest x1 16.3 us: on_device(): jnp.zeros((group_points,), jnp.float32).at[visit_point]]
  transfers between devices with their start and end apart: 4 -> 0, of which waited for: 1 -> 0; matrix products, arithmetic and copies ran while one was open for 2% -> 0% of each run, Pallas kernels for 0% -> 0%
where the time goes in v1:
time: 128 us; the launch traced here: 127 us
  Pallas kernels  111 us (87%)
  local copies, waits for them, and re-layouts  8.06 us (6%)
  other arithmetic  7.06 us (6%)
    pallas_call x1, Pallas kernels, on_device(): pl.pallas_call(functools.partial(exchange_kernel, peers, shells), in_spec...  48.2 us
    pallas_call x1, Pallas kernels, on_device(): pl.pallas_call(functools.partial(thread_kernel, peers), in_specs=[vmem] *...  26.9 us
    pallas_call x1, Pallas kernels, on_device(): pl.pallas_call(step_kernel, out_shape=[shape((fields, blocks, cells), F32...  20.2 us
    pallas_call x1, Pallas kernels, on_device(): pl.pallas_call(pack_kernel, out_shape=[shape((fields, 8, 64, blocks), F32...  12.2 us
    reduce_max x1, other arithmetic, targets(): lone = jnp.max(column, axis=1, keepdims=True)  4.4 us
    pallas_call x1, Pallas kernels, on_device(): pl.pallas_call(write_kernel, grid=(1,), in_specs=[plane, whole((peers, 8,...  3.68 us

profile of v1, /device:TPU:0, one launch (start us, length us, event | category | flops | bytes accessed | tf_op | source)
XLA Modules:
  0.0 127.2 jit_solution(9979584517940377315)
XLA Ops:
  0.6 0.9 compare_reduce_fusion
  1.5 0.1 eq.52
  1.6 0.1 eq.54
  1.7 0.1 eq.56
  1.8 1.0 slice_reduce_fusion
  2.8 0.1 squeeze.2
  3.0 0.1 concatenate.13
  3.1 0.6 reshape.85.copt
  3.7 0.1 pad.1.clone
  3.8 0.1 pad.2.clone
  3.9 0.6 convert_element_type.11.ccode
  4.5 0.1 select_n.54
  4.6 0.1 concatenate.12
  4.7 0.6 reshape.84.cidx
  5.3 1.3 %reshape.86.vp = s32[8,512]{1,0:T(8,128)} reshape(s32[4096]{0:T(1024)} %param.12) | data formatting | bytes 32768 | tf_op jit(solution)/shard_map/reshape | solution.py:555
  6.6 12.2 %pack.1 = (f32[8,8,64,128]{3,2,1,0:T(8,128)}, f32[32,136,128]{2,1,0:T(8,128)}, f32[3,128]{1,0:T(4,128)}, f32[8,128]{1,0:T(8,128)}) custom-call(f32[8,128,512]{2,1,0:T(8,128)} %state.1, f32[3,8,8,128]{3,2,1,0:T(8,128)} %jac.3, s32[16,256]{1,0:T(8,128)} %reshape.84.cidx, s32[16,256]{1,0:T(8,128)} %reshape.85.copt, f32[16,256]{1,0:T(8,128)} %convert_element_type.11.ccode, ...), custom_call_target="tpu_custom_call" | custom-call | tf_op jit(solution)/shard_map/pack/pallas_call | solution.py:558
  18.8 0.0 copy-start
  18.8 48.2 %exchange.1 = (f32[32,136,128]{2,1,0:T(8,128)}, f32[8,64,128]{2,1,0:T(8,128)}, f32[8,64,128]{2,1,0:T(8,128)}, f32[8,128]{1,0:T(8,128)}) custom-call(f32[32,136,128]{2,1,0:T(8,128)} %get-tuple-element.15.slabs, f32[8,8,64,128]{3,2,1,0:T(8,128)} %get-tuple-element.16.u, f32[8,128]{1,0:T(8,128)} %get-tuple-element.17.wmax), custom_call_target="tpu_custom_call" | custom-call | tf_op jit(solution)/shard_map/exchange/pallas_call | solution.py:572
  67.1 0.0 copy-start.1
  67.1 0.0 copy-done
  67.1 0.3 div.13
  67.5 0.4 rem.22
  67.8 0.3 lt.31
  68.1 0.3 ne.30
  68.4 4.4 %fusion.5 = (s32[4,128]{0,1:T(8,128)S(1)}, s32[4,4,128]{1,0,2:T(4,128)S(1)}, s32[4,128]{0,1:T(8,128)S(1)}) fusion(s32[128,4,4]{2,1,0:T(4,128)S(1)} %div.13, s32[128,4,4]{2,1,0:T(4,128)S(1)} %rem.22, pred[128,4,4]{2,1,0:T(4,128)(4,1)S(1)} %ne.30, pred[128,4,4]{2,1,0:T(4,128)(4,1)S(1)} %lt.31), kind=kLoop, calls=%fused_computation.29 | loop fusion | flops 27648 | bytes 32768 | tf_op jit(solution)/shard_map/reduce_max | solution.py:540
  72.9 0.7 select_select_fusion
  73.6 0.7 copy.11
  74.3 0.0 copy-done.1
  74.3 0.6 reshape.88.vc
  75.0 0.0 copy-start.3
  75.0 20.2 %step.1 = (f32[8,128,512]{2,1,0:T(8,128)}, f32[8,512]{1,0:T(8,128)}, f32[32,8,128]{2,1,0:T(8,128)}, f32[32,8,128]{2,1,0:T(8,128)}) custom-call(f32[32,136,128]{2,1,0:T(8,128)} %get-tuple-element.18.recv, s32[1,2048]{1,0:T(1,128)} %bitcast.29, f32[8,8,64,128]{3,2,1,0:T(8,128)} %get-tuple-element.16.u, f32[8,64,128]{2,1,0:T(8,128)} %get-tuple-element.19.lower, ...), custom_call_target="tpu_custom_call" | custom-call | tf_op jit(solution)/shard_map/step/pallas_call | solution.py:600
  95.2 0.0 copy-done.3
  95.2 0.8 copy.12.lengths
  96.0 26.9 %threads.1 = (f32[8,512]{1,0:T(8,128)}, f32[32,8,128]{2,1,0:T(8,128)}) custom-call(f32[32,8,128]{2,1,0:T(8,128)} %get-tuple-element.24.outgoing, f32[32,8,128]{2,1,0:T(8,128)} %get-tuple-element.25.tidx, f32[256,512]{1,0:T(8,128)} %conductance.1, s32[256,1]{1,0:T(8,128)} %copy.12.lengths), custom_call_target="tpu_custom_call" | custom-call | tf_op jit(solution)/shard_map/threads/pallas_call | solution.py:619
  122.9 0.0 copy-start.2
  122.9 3.7 %write.1 = f32[8,128,512]{2,1,0:T(8,128)} custom-call(f32[8,128,512]{2,1,0:T(8,128)} %get-tuple-element.23.old, f32[32,8,128]{2,1,0:T(8,128)} %get-tuple-element.26.returned, s32[8,512]{1,0:T(8,128)} %reshape.88.vc, s32[8,512]{1,0:T(8,128)} %reshape.86.vp), custom_call_target="tpu_custom_call", output_to_operand_aliasing={{}: (0, {})} | custom-call | tf_op jit(solution)/shard_map/write/pallas_call | solution.py:641
  126.6 0.0 copy-done.2
  126.6 0.6 copy.15
  (14 shorter events, 0.1 us)
Async XLA Ops:
  18.8 48.2 %copy-start = (s32[2048]{0:T(1024)S(1)}, s32[2048]{0:T(1024)}, u32[]{:S(2)}) copy-start(s32[2048]{0:T(1024)} %param.11) | copy-start | bytes 24580
  67.1 7.3 %copy-start.1 = (s32[4096]{0:T(1024)S(1)}, s32[4096]{0:T(1024)}, u32[]{:S(2)}) copy-start(s32[4096]{0:T(1024)} %param.13) | copy-start | bytes 49156
  75.0 20.2 %copy-start.3 = (s32[256]{0:T(256)S(1)}, s32[256]{0:T(256)}, u32[]{:S(2)}) copy-start(s32[256]{0:T(256)} %param.15) | copy-start | bytes 3076
  122.9 3.7 %copy-start.2 = (f32[8,512]{1,0:T(8,128)S(1)}, f32[8,512]{1,0:T(8,128)}, u32[]{:S(2)}) copy-start(f32[8,512]{1,0:T(8,128)} %get-tuple-element.47) | copy-start | bytes 49156

commit v2 on v0

v2 whole, which is shorter than its diff:
```python
import functools

import jax
import jax.numpy as jnp
from jax import lax
from jax.experimental import pallas as pl
from jax.experimental.pallas import tpu as pltpu
from jax.sharding import PartitionSpec as P

BS = 8
FULL = 17
CAP = 70
PEERS = 32
SHELLS = 4
CFL_NUMBER = 0.3
MESH = pl.DeviceIdType.MESH
F32 = jnp.float32
BF16 = jnp.bfloat16
VMEM_BYTES = 60 * 1024 * 1024


def iota(shape, dim):
    return lax.broadcasted_iota(jnp.int32, shape, dim)


def one_hot(mask):
    return jnp.where(mask, 1.0, 0.0).astype(BF16)


def high_low(x):
    high = x.astype(BF16).astype(F32)
    return high, x - high


def half_roll(x):
    shape = x.shape
    return pltpu.roll(x.reshape(-1, 8, 128), 4, 1).reshape(shape)


def rows_to_lanes(ref, *lead):
    return jnp.concatenate([ref[(*lead, slice(c, c + 1))] for c in range(4)], axis=1)


def lanes_to_rows(line):
    return [line[:, c * 128 : (c + 1) * 128] for c in range(4)]


def partner(me, n, sign):
    offset = lax.rem(11 * n, PEERS)
    dy, dz, dx = lax.div(offset, 8), lax.rem(lax.div(offset, 4), 2), lax.rem(offset, 4)
    y, z, x = lax.div(me, 8), lax.rem(lax.div(me, 4), 2), lax.rem(me, 4)
    y = lax.rem(y + 4 + sign * dy, 4)
    z = lax.rem(z + dz, 2)
    x = lax.rem(x + 4 + sign * dx, 4)
    return y * 8 + z * 4 + x


def column_plan(plan, cidx, copt, ccode):
    word = plan[...]
    row, level, quad = word & 511, (word >> 9) & 3, (word >> 11) & 3
    lane = iota(word.shape, 1)
    row = jnp.where((level == 3) | (lane >= CAP), -1, row)
    option = jnp.where(level == 1, quad, jnp.where(level == 2, 4, 0))
    code = jnp.where(level == 0, 16, jnp.where(level == 1, 32, jnp.where(level == 2, 1 + quad, 0)))
    code = jnp.where(lane < CAP, code, 0)
    index = row
    for q in range(1, 4):
        start = CAP + FULL * (q - 1)
        here = (lane >= start) & (lane < start + FULL)
        index = jnp.where(here, pltpu.roll(row, start, 1), index)
        option = jnp.where(here, q, option)
    cidx[...] = index
    copt[...] = option
    ccode[...] = code.astype(F32)


def column_targets(named, tgt):
    value = named[...]
    sender = (value * 59919) >> 22
    column = jnp.where(value < PEERS * CAP, value + sender * (128 - CAP), -1)
    for j in range(4):
        rows = [column[j * 4 + e : j * 4 + e + 1, :] for e in range(4)]
        used = [jnp.where(row >= 0, 1, 0) for row in rows]
        single = used[0] + used[1] + used[2] + used[3] == 1
        lone = jnp.maximum(jnp.maximum(rows[0], rows[1]), jnp.maximum(rows[2], rows[3]))
        for e in range(4):
            if e == 0:
                other = lone
            else:
                other = jnp.where((lone & 127) < FULL, lone + CAP + FULL * (e - 1), -1)
            lanes = slice((j * 4 + e) * 128, (j * 4 + e + 1) * 128)
            tgt[:, lanes] = jnp.where(single, other, rows[e])


def build_table(u, table, mean):
    low_half = iota((1, 1, 1, 8, 128), 3) < 4
    for j in range(4):
        if j == 0:
            face = u[:, 1:9, 8:16, :]
        elif j == 1:
            face = u[:, 1:9, 64:72, :]
        else:
            face = u[:, 1:9, pl.ds(8 if j == 2 else 15, 8, stride=8), :]
        parts = face.reshape(8, 2, 2, 2, 8, 128)
        first, second = parts[:, :, :, 0], parts[:, :, :, 1]
        left = jnp.where(low_half, first, half_roll(second))
        right = jnp.where(low_half, half_roll(first), second)
        lanes = slice(j * 128, (j + 1) * 128)
        pairs = face.reshape(8, 4, 2, 8, 128)
        mean[...] = (pairs[:, :, 0] + pairs[:, :, 1]).reshape(256, 128)
        rest = 0.25 * (mean[pl.ds(0, 128, stride=2), :] + mean[pl.ds(1, 128, stride=2), :])
        options = [
            left[:, 0].reshape(128, 128),
            right[:, 0].reshape(128, 128),
            left[:, 1].reshape(128, 128),
            right[:, 1].reshape(128, 128),
            rest,
        ]
        for option, rows in enumerate(options):
            high, low = high_low(rows)
            table[option * 128 : (option + 1) * 128, lanes] = high.astype(BF16)
            table[640 + option * 128 : 768 + option * 128, lanes] = low.astype(BF16)


def inner_step(u, jac, ws, change):
    inner = iota((2, 8, 128), 1)

    def cell(n, carry):
        r, pair = lax.div(n, 4), lax.rem(n, 4)
        a = pair * 2
        rows = pl.ds(pl.multiple_of(a * 8 + 8, 8), 16)
        own = [u[h, r + 1, rows, :].reshape(2, 8, 128) for h in range(8)]
        total = [jnp.zeros((2, 8, 128), F32) for _ in range(8)]
        for d in range(3):
            gap = []
            speed = ws[d : d + 1, :].reshape(1, 1, 128)
            for h in range(8):
                if d == 0:
                    below = u[h, r, rows, :].reshape(2, 8, 128)
                    above = u[h, r + 2, rows, :].reshape(2, 8, 128)
                elif d == 1:
                    below = u[h, r + 1, pl.ds(pl.multiple_of(a * 8, 8), 16), :].reshape(2, 8, 128)
                    above = u[h, r + 1, pl.ds(pl.multiple_of(a * 8 + 16, 8), 16), :].reshape(2, 8, 128)
                else:
                    below = jnp.where(inner == 0, 0.0, pltpu.roll(own[h], 1, 1))
                    above = jnp.where(inner == 7, 0.0, pltpu.roll(own[h], 7, 1))
                gap.append(above - below)
                total[h] = total[h] - speed * (above - 2.0 * own[h] + below)
            for g in range(8):
                for h in range(8):
                    total[g] = total[g] + jac[d, g, h : h + 1, :].reshape(1, 1, 128) * gap[h]
        for g in range(8):
            change[g, r, pl.ds(pl.multiple_of(a * 8, 8), 16), :] = total[g].reshape(16, 128)
        return carry

    lax.fori_loop(0, 32, cell, 0)


def add_ghosts(g, ghosts, jac, ws, change):
    for j in range(4):
        d = 1 + j // 2
        flux = jnp.zeros((8, 8, 128), F32)
        for h in range(8):
            flux = flux + jac[d, pl.ds(g, 1), pl.ds(h, 1), :].reshape(1, 1, 128) * ghosts[j, h]
        spread = ws[d : d + 1, :].reshape(1, 1, 128) * ghosts[j, pl.ds(g, 1)].reshape(8, 8, 128)
        part = (flux if j % 2 else -flux) - spread
        if j < 2:
            rows = pl.ds(56 * j, 8)
        else:
            rows = pl.ds(7 * (j - 2), 8, stride=8)
        here = change[pl.ds(g, 1), :, rows, :].reshape(8, 8, 128)
        change[pl.ds(g, 1), :, rows, :] = (here + part).reshape(1, 8, 8, 128)


def advance_field(g, u, change, ratio, plain):
    new = u[pl.ds(g, 1), 1:9, 8:72, :] - ratio * change[pl.ds(g, 1)]
    plain[pl.ds(g, 1)] = new.reshape(512, 128).T.reshape(1, 128, 512)


def ghost_layers(acc, ghosts, spread):
    low_half = iota((1, 1, 8, 128), 2) < 4
    for j in range(4):
        values, codes = [], []
        for e in range(4):
            lanes = slice((j * 4 + e) * 128, (j * 4 + e + 1) * 128)
            values.append(acc[0:128, lanes] + acc[128:256, lanes])
            codes.append(acc[256:257, lanes])
        whole = codes[0] == 16.0
        coarse = (codes[0] == 32.0).reshape(1, 1, 1, 128)
        spread[pl.ds(0, 128, stride=2), :] = values[0]
        spread[pl.ds(1, 128, stride=2), :] = values[0]
        for i in range(2):
            quads = []
            for q in (2 * i, 2 * i + 1):
                fine = jnp.zeros((128, 128), F32)
                for e in range(4):
                    fine = jnp.where(codes[e] == 1.0 + q, values[e], fine)
                quads.append(jnp.where(whole, values[q], fine).reshape(8, 2, 8, 128))
            left, right = quads
            first = jnp.where(low_half, left, half_roll(right))
            second = jnp.where(low_half, half_roll(left), right)
            repeated = spread[...].reshape(8, 4, 8, 128)[:, 2 * i : 2 * i + 2]
            first = jnp.where(coarse, repeated, first)
            second = jnp.where(coarse, repeated, second)
            for xp in range(2):
                ghosts[j, :, 4 * i + 2 * xp] = first[:, xp]
                ghosts[j, :, 4 * i + 2 * xp + 1] = second[:, xp]


def reduce_threads(weight, rhs):
    left, right = pltpu.roll(weight, 1, 1), weight
    excess = jnp.ones_like(weight)
    points = weight.shape[1]
    stride = 1
    while stride < points:
        inv = 1.0 / (excess + left + right)
        e, r = excess * inv, rhs * inv
        back, ahead = stride, points - stride
        new_excess = excess + left * pltpu.roll(e, back, 1) + right * pltpu.roll(e, ahead, 1)
        rhs = rhs + left * pltpu.roll(r, back, 1) + right * pltpu.roll(r, ahead, 1)
        left, right = (
            left * pltpu.roll(left * inv, back, 1),
            right * pltpu.roll(right * inv, ahead, 1),
        )
        excess = new_excess
        stride *= 2
    return rhs / (excess + left + right)


def whole_kernel(
    state, jac, plan, named, vp, vc, conductance, lengths,
    new_state, thread_temp,
    plain, u, lower, upper, table, mean, cidx, copt, ccode, tgt, slabs, recv, shell_max, own_max,
    columns, acc, ghosts, change, ws, cells, picks, rows_of, weights, outgoing, arrived, back, returned,
    state_sem, rim_send, rim_recv, shell_send, shell_recv, slab_send, slab_recv,
    out_send, out_recv, back_send, back_recv, local_sem, write_sem,
):
    me = lax.axis_index("blk")
    shell = lax.axis_index("shell")
    barrier = pltpu.get_barrier_semaphore()

    loads = [pltpu.make_async_copy(state.at[f], plain.at[f], state_sem.at[f]) for f in range(8)]
    for load in loads:
        load.start()
    weight_load = pltpu.make_async_copy(
        conductance.at[pl.ds(pl.multiple_of(me * 8, 8), 8)], weights, local_sem.at[0]
    )
    weight_load.start()

    def greet(n, carry):
        pl.semaphore_signal(barrier, inc=1, device_id={"blk": partner(me, n, 1)}, device_id_type=MESH)
        return carry

    lax.fori_loop(1, PEERS, greet, 0)
    for d in range(1, SHELLS):
        pl.semaphore_signal(
            barrier, inc=1, device_id={"shell": lax.rem(shell + d, SHELLS)}, device_id_type=MESH
        )

    speed = jnp.max(jnp.sum(jnp.abs(jac[...]), axis=2), axis=1)
    ws[...] = speed
    own_max[...] = jnp.broadcast_to(jnp.max(speed), (8, 128))
    column_plan(plan, cidx, copt, ccode)
    column_targets(named, tgt)
    u[:, :, 0:8, :] = jnp.zeros((8, 10, 8, 128), F32)
    u[:, :, 72:80, :] = jnp.zeros((8, 10, 8, 128), F32)

    for f in range(8):
        loads[f].wait()
        u[f, 1:9, 8:72, :] = plain[f].T.reshape(8, 64, 128)

    pl.semaphore_wait(barrier, PEERS + SHELLS - 2)

    def shell_copy(d):
        return pltpu.make_async_remote_copy(
            src_ref=own_max, dst_ref=shell_max.at[d], send_sem=shell_send.at[d],
            recv_sem=shell_recv.at[d],
            device_id={"shell": lax.rem(shell + d, SHELLS)}, device_id_type=MESH,
        )

    for d in range(1, SHELLS):
        shell_copy(d).start()

    def rim_up():
        return pltpu.make_async_remote_copy(
            src_ref=u.at[:, 8, 8:72], dst_ref=lower, send_sem=rim_send.at[0], recv_sem=rim_recv.at[0],
            device_id={"shell": lax.rem(shell + 1, SHELLS)}, device_id_type=MESH,
        )

    def rim_down():
        return pltpu.make_async_remote_copy(
            src_ref=u.at[:, 1, 8:72], dst_ref=upper, send_sem=rim_send.at[1], recv_sem=rim_recv.at[1],
            device_id={"shell": lax.rem(shell + SHELLS - 1, SHELLS)}, device_id_type=MESH,
        )

    @pl.when(shell < SHELLS - 1)
    def _():
        rim_up().start()

    @pl.when(shell > 0)
    def _():
        rim_down().start()

    build_table(u, table, mean)
    points = jnp.concatenate([vp[pl.ds(c, 8, stride=4), :] for c in range(4)], axis=1)
    used = points < 256 * 512
    owner = jnp.max(jnp.where(used, points >> 12, -1), axis=1, keepdims=True)
    local = jnp.where(used, points & 4095, -1).astype(F32) + 1.0
    best = own_max[...]
    for d in range(1, SHELLS):
        shell_copy(d).wait()
        best = jnp.maximum(best, shell_max[d])

    def slab_copy(n, sign):
        peer = partner(me, n, 1)
        slot = me if sign > 0 else partner(me, n, -1)
        return pltpu.make_async_remote_copy(
            src_ref=slabs.at[peer], dst_ref=recv.at[slot],
            send_sem=slab_send.at[n], recv_sem=slab_recv.at[n],
            device_id={"blk": peer}, device_id_type=MESH,
        )

    def pack(i, carry):
        pair = [partner(me, 2 * i, 1), partner(me, 2 * i + 1, 1)]
        index = jnp.concatenate([cidx[pl.ds(p, 1), :] for p in pair], axis=1)
        option = jnp.concatenate([copt[pl.ds(p, 1), :] for p in pair], axis=1)
        picked = one_hot(iota((512, 256), 0) == index)
        got = jnp.dot(table[...], picked, preferred_element_type=F32)
        chosen = got[0:128] + got[640:768]
        for o in range(1, 5):
            chosen = jnp.where(
                option == o, got[o * 128 : (o + 1) * 128] + got[640 + o * 128 : 768 + o * 128], chosen
            )
        for half in range(2):
            peer = pair[half]
            slabs[peer, 0:128, :] = chosen[:, half * 128 : half * 128 + 128]
            run = jnp.sum(jnp.where(owner == peer, local, 0.0), axis=0, keepdims=True) - 1.0
            rows = [ccode[pl.ds(peer, 1), :]] + lanes_to_rows(run) + [best[0:1, :], jnp.zeros((2, 128), F32)]
            slabs[peer, 128:136, :] = jnp.concatenate(rows, axis=0)
            if half == 0:

                @pl.when(i > 0)
                def _():
                    slab_copy(2 * i, 1).start()

            else:
                slab_copy(2 * i + 1, 1).start()
        return carry

    lax.fori_loop(0, PEERS // 2, pack, 0)
    recv[me] = slabs[me]

    @pl.when(shell > 0)
    def _():
        rim_up().wait_recv()
        u[:, 0, 8:72, :] = lower[...]

    @pl.when(shell == 0)
    def _():
        u[:, 0, 8:72, :] = u[:, 1, 8:72, :]

    @pl.when(shell < SHELLS - 1)
    def _():
        rim_down().wait_recv()
        u[:, 9, 8:72, :] = upper[...]

    @pl.when(shell == SHELLS - 1)
    def _():
        u[:, 9, 8:72, :] = u[:, 8, 8:72, :]

    inner_step(u, jac, ws, change)

    def columns_of(n, carry):
        wanted = tgt[...] - partner(me, n, -1) * 128
        columns[pl.ds(pl.multiple_of(n * 128, 128), 128), :] = one_hot(iota((128, 2048), 0) == wanted)
        return carry

    lax.fori_loop(0, PEERS, columns_of, 0)
    where_to = jnp.concatenate([vc[pl.ds(c, 8, stride=4), :] for c in range(4)], axis=1)
    for run in range(8):
        cells[run] = one_hot(iota((512, 512), 0) == (where_to[run : run + 1, :] & 511))

    def arrive(i, top):
        tiles = []
        for k in range(4):
            n = 4 * i + k
            if k == 0:

                @pl.when(i > 0)
                def _():
                    slab_copy(n, -1).wait()

            else:
                slab_copy(n, -1).wait()
            slab = recv[partner(me, n, -1)]
            high, low = high_low(slab[0:128])
            tiles.append(
                jnp.concatenate([low, high, slab[128:136], jnp.zeros((8, 128), F32)], axis=0).astype(BF16)
            )
            top = jnp.maximum(top, slab[133:134])
        rows = jnp.concatenate(tiles, axis=1)
        for n in range(4):
            lanes = slice(n * 512, (n + 1) * 512)
            part = jnp.dot(
                rows, columns[pl.ds(pl.multiple_of(i * 512, 512), 512), lanes], preferred_element_type=F32
            )
            acc[:, lanes] = acc[:, lanes] + part
        return top

    acc[...] = jnp.zeros_like(acc)
    top = lax.fori_loop(0, PEERS // 4, arrive, jnp.zeros((1, 128), F32))
    ghost_layers(acc, ghosts, spread=mean)
    ratio = (0.5 * (CFL_NUMBER / top)).reshape(1, 1, 1, 128)

    add_ghosts(7, ghosts, jac, ws, change)
    advance_field(7, u, change, ratio, plain)
    high, low = high_low(plain[7])
    rows = jnp.concatenate([high, low], axis=0).astype(BF16)
    block = where_to >> 9
    total = jnp.zeros((PEERS, 512), F32)
    for run in range(8):
        got = jnp.dot(rows, cells[run], preferred_element_type=F32)
        got = got[0:128] + got[128:256]
        line = jnp.sum(
            jnp.where(iota((128, 512), 0) == block[run : run + 1, :], got, 0.0), axis=0, keepdims=True
        )
        total = jnp.where(iota((PEERS, 512), 0) == owner[run : run + 1, :], line, total)
    outgoing[...] = jnp.zeros_like(outgoing)
    for c in range(4):
        outgoing[:, c, :] = total[:, c * 128 : (c + 1) * 128]

    def line_copy(src, dst, n, sign, ssem, rsem):
        peer = partner(me, n, 1)
        slot = me if sign > 0 else partner(me, n, -1)
        return pltpu.make_async_remote_copy(
            src_ref=src.at[peer], dst_ref=dst.at[slot], send_sem=ssem.at[n], recv_sem=rsem.at[n],
            device_id={"blk": peer}, device_id_type=MESH,
        )

    def send_out(n, carry):
        line_copy(outgoing, arrived, n, 1, out_send, out_recv).start()
        return carry

    lax.fori_loop(1, PEERS, send_out, 0)
    arrived[me] = outgoing[me]

    def prepare(i, carry):
        for k in range(4):
            lanes = slice(k * 512, (k + 1) * 512)
            s = partner(me, 4 * i + k, -1)
            point = jnp.concatenate([recv[s, 129 + c : 130 + c, :] for c in range(4)], axis=1).astype(jnp.int32)
            picks[i, :, lanes] = one_hot(iota((128, 512), 0) == (point & 127))
            row = ((point >> 7) & 3) * 8 + (point >> 9)
            rows_of[i, :, lanes] = jnp.broadcast_to(jnp.where(point < 0, -1, row), (8, 512))
        return carry

    lax.fori_loop(0, PEERS // 4, prepare, 0)

    writes = [pltpu.make_async_copy(plain.at[f], new_state.at[f], write_sem.at[f]) for f in range(8)]

    def other_field(g, carry):
        add_ghosts(g, ghosts, jac, ws, change)
        advance_field(g, u, change, ratio, plain)
        return carry

    lax.fori_loop(0, 3, other_field, 0)
    for f in range(3):
        writes[f].start()

    def collect(i, total):
        parts = []
        for k in range(4):
            n = 4 * i + k
            s = partner(me, n, -1)
            if k == 0:

                @pl.when(i > 0)
                def _():
                    line_copy(outgoing, arrived, n, -1, out_send, out_recv).wait()

            else:
                line_copy(outgoing, arrived, n, -1, out_send, out_recv).wait()
            high, low = high_low(rows_to_lanes(arrived, s))
            mask = iota((32, 512), 0) == rows_of[i, 0:1, k * 512 : (k + 1) * 512]
            parts.append(
                jnp.concatenate([jnp.where(mask, high, 0.0), jnp.where(mask, low, 0.0)], axis=0).astype(BF16)
            )
        return total + lax.dot_general(
            jnp.concatenate(parts, axis=1), picks[i], (((1,), (1,)), ((), ())), preferred_element_type=F32
        )

    total = lax.fori_loop(0, PEERS // 4, collect, jnp.zeros((64, 128), F32))
    total = total[0:32] + total[32:64]
    rhs = jnp.concatenate([total[c * 8 : (c + 1) * 8] for c in range(4)], axis=1)
    first = me * 8
    here = iota((8, 128), 1) == lax.rem(first, 128) + iota((8, 128), 0)
    length = jnp.sum(jnp.where(here, lengths[pl.ds(lax.div(first, 128), 1), :], 0), axis=1, keepdims=True)
    weight_load.wait()
    weight = jnp.where(iota((8, 512), 1) + 1 < length, weights[...], 0.0)
    solved = reduce_threads(weight, rhs)
    thread_temp[...] = solved
    high, low = high_low(solved)
    answers = jnp.concatenate(lanes_to_rows(high) + lanes_to_rows(low), axis=0).astype(BF16)

    def answer(i, carry):
        got = jnp.dot(answers, picks[i], preferred_element_type=F32)
        got = got[0:32] + got[32:64]
        mask = iota((32, 2048), 0) == rows_of[i, 0:1, :]
        line = jnp.sum(jnp.where(mask, got, 0.0), axis=0, keepdims=True)
        for k in range(4):
            n = 4 * i + k
            part = lanes_to_rows(line[:, k * 512 : (k + 1) * 512])
            back[partner(me, n, -1)] = jnp.concatenate(part + [jnp.zeros((4, 128), F32)], axis=0)
        return carry

    lax.fori_loop(0, PEERS // 4, answer, 0)

    def send_back(n, carry):
        line_copy(back, returned, n, 1, back_send, back_recv).start()
        return carry

    lax.fori_loop(1, PEERS, send_back, 0)
    returned[me] = back[me]

    lax.fori_loop(3, 7, other_field, 0)
    for f in range(3, 7):
        writes[f].start()

    visited = jnp.where(used, block, -1)
    cover = jnp.zeros((128, 512), F32)
    for run in range(8):
        mask = one_hot(iota((128, 512), 0) == visited[run : run + 1, :])
        cover = cover + lax.dot_general(
            mask, cells[run], (((1,), (1,)), ((), ())), preferred_element_type=F32
        )

    def get_back(n, carry):
        line_copy(back, returned, n, -1, back_send, back_recv).wait()
        return carry

    lax.fori_loop(1, PEERS, get_back, 0)
    values = jnp.zeros((8, 512), F32)
    for o in range(PEERS):
        values = jnp.where(owner == o, rows_to_lanes(returned, o), values)
    high, low = high_low(values)
    total = jnp.zeros((256, 512), F32)
    for run in range(8):
        mask = iota((128, 512), 0) == visited[run : run + 1, :]
        rows = jnp.concatenate(
            [jnp.where(mask, high[run : run + 1, :], 0.0), jnp.where(mask, low[run : run + 1, :], 0.0)], axis=0
        ).astype(BF16)
        total = total + lax.dot_general(
            rows, cells[run], (((1,), (1,)), ((), ())), preferred_element_type=F32
        )
    plain[7] = jnp.where(cover > 0.5, total[0:128] + total[128:256], plain[7])
    writes[7].start()
    for write in writes:
        write.wait()

    @pl.when(shell < SHELLS - 1)
    def _():
        rim_up().wait_send()

    @pl.when(shell > 0)
    def _():
        rim_down().wait_send()


def on_device(
    plasma_state, jacobian, send_list, recv_map, visit_point, visit_cell, conductance, lengths
):
    fields, blocks, cells = plasma_state.shape
    block, face, level, quad = send_list[0], send_list[1], send_list[2], send_list[3]
    plan = (block + 128 * face + 512 * level + 2048 * quad).reshape(PEERS, CAP)
    plan = jnp.pad(plan, ((0, 0), (0, 128 - CAP)))
    named = recv_map.reshape(blocks, 16).T
    shape = jax.ShapeDtypeStruct
    vmem = pl.BlockSpec(memory_space=pltpu.VMEM)
    anywhere = pl.BlockSpec(memory_space=pl.ANY)
    dma = lambda n: pltpu.SemaphoreType.DMA((n,))
    buffer = lambda *dims: pltpu.VMEM(dims, F32)
    new_state, thread_temp = pl.pallas_call(
        whole_kernel,
        in_specs=[anywhere, vmem, vmem, vmem, vmem, vmem, anywhere, vmem],
        out_specs=[anywhere, vmem],
        out_shape=[shape((fields, blocks, cells), F32), shape((8, 512), F32)],
        scratch_shapes=[
            buffer(fields, blocks, cells),
            buffer(fields, 10, 80, 128),
            buffer(fields, 64, 128),
            buffer(fields, 64, 128),
            pltpu.VMEM((1280, 512), BF16),
            buffer(256, 128),
            pltpu.VMEM((PEERS, 128), jnp.int32),
            pltpu.VMEM((PEERS, 128), jnp.int32),
            buffer(PEERS, 128),
            pltpu.VMEM((1, 2048), jnp.int32),
            buffer(PEERS, 136, 128),
            buffer(PEERS, 136, 128),
            buffer(SHELLS, 8, 128),
            buffer(8, 128),
            pltpu.VMEM((PEERS * 128, 2048), BF16),
            buffer(272, 2048),
            buffer(4, fields, 8, 8, 128),
            buffer(fields, 8, 64, 128),
            buffer(3, 128),
            pltpu.VMEM((8, 512, 512), BF16),
            pltpu.VMEM((8, 128, 2048), BF16),
            pltpu.VMEM((8, 8, 2048), jnp.int32),
            buffer(8, 512),
            buffer(PEERS, 8, 128),
            buffer(PEERS, 8, 128),
            buffer(PEERS, 8, 128),
            buffer(PEERS, 8, 128),
            dma(8), dma(2), dma(2), dma(SHELLS), dma(SHELLS), dma(PEERS), dma(PEERS),
            dma(PEERS), dma(PEERS), dma(PEERS), dma(PEERS), dma(1), dma(8),
        ],
        compiler_params=pltpu.CompilerParams(
            vmem_limit_bytes=VMEM_BYTES, collective_id=1, has_side_effects=True
        ),
        name="mhd_step",
    )(
        plasma_state, jacobian, plan, named, visit_point.reshape(-1, 128), visit_cell.reshape(-1, 128),
        conductance, lengths.reshape(-1, 128),
    )
    return (new_state, thread_temp)


def solution(mesh):
    in_specs = (
        P(None, ("shell", "blk"), None),
        P(None, None, None, ("shell", "blk")),
        P(None, ("shell", "blk")),
        P(("shell", "blk")),
        P(("shell", "blk")),
        P(("shell", "blk")),
        P("shell", None),
        P("shell"),
    )
    out_specs = (P(None, ("shell", "blk"), None), P(("shell", "blk"), None))
    return jax.shard_map(
        on_device, mesh=mesh, in_specs=in_specs, out_specs=out_specs, check_vma=False
    )
```

time: 1030 us -> 77.1 us (0.07)
  waiting for transfers between devices: 346 us -> 0 us
  local copies, waits for them, and re-layouts: 320 us -> 5.85 us
  blocking collectives: 197 us -> 0 us
  matrix products: 72.7 us -> 0 us
  Pallas kernels: 0 us -> 69.3 us
  other arithmetic: 56.5 us -> 0.99 us
  starting transfers between devices: 16 us -> 0 us
  between operations: 16.3 us -> 0.66 us
    unnamed x2 -> x0, waiting for transfers between devices: 346 us -> none
    broadcast_in_dim x1535 -> x0, local copies, waits for them, and re-layouts: 124 us -> none  [the longest x1534 124 us: thread_solve(): lax.linalg.tridiagonal_solve(-before, diagonal, -link_weight, samples[:,...]
    pmax x1 -> x0, blocking collectives: 99.7 us -> none  [on_device(): fastest = lax.pmax(jnp.max(wave_speed), ('shell', 'blk'))]
    all_gather x1 -> x0, blocking collectives: 96.9 us -> none  [on_device(): lax.all_gather(thread_temp.reshape(-1), 'blk', axis=0, tiled=True)]
    gather x4 -> x0, local copies, waits for them, and re-layouts: 73.3 us -> none  [the longest x1 23 us: on_device(): sampled = pressure[visit_cell]]
    dot_general x9 -> x0, matrix products: 72.7 us -> none  [the longest x1 41.6 us: select_apply(): product = jnp.einsum('fpc,cm->fpm', rows, table, precision=HIGH)]
    pallas_call x0 -> x1, Pallas kernels: none -> 69.3 us  [on_device(): pl.pallas_call(whole_kernel, in_specs=[anywhere, vmem, vmem, vmem, vmem,...]
    scatter x3 -> x0, local copies, waits for them, and re-layouts: 34.2 us -> none  [the longest x1 16.3 us: on_device(): jnp.zeros((group_points,), jnp.float32).at[visit_point]]
  transfers between devices with their start and end apart: 4 -> 0, of which waited for: 1 -> 0; matrix products, arithmetic and copies ran while one was open for 2% -> 0% of each run, Pallas kernels for 0% -> 0%
where the time goes in v2:
time: 77.1 us; the launch traced here: 76.8 us
  Pallas kernels  69.3 us (90%)
  local copies, waits for them, and re-layouts  5.85 us (8%)
  other arithmetic  0.99 us (1%)
    pallas_call x1, Pallas kernels, on_device(): pl.pallas_call(whole_kernel, in_specs=[anywhere, vmem, vmem, vmem, vmem,...  69.3 us
    unnamed x4, local copies, waits for them, and re-layouts  3.69 us

profile of v2, /device:TPU:0, one launch (start us, length us, event | category | flops | bytes accessed | tf_op | source)
XLA Modules:
  0.0 76.8 jit_solution(11198743657618297645)
XLA Ops:
  0.6 1.0 %add_reduce_fusion = s32[2240]{0:T(1024)S(1)} fusion(s32[4,2240]{1,0:T(4,128)} %param.10), kind=kLoop, calls=%fused_computation | loop fusion | flops 13440 | bytes 44800 | tf_op jit(solution)/shard_map/add | solution.py:574
  1.6 0.1 add.22
  1.7 0.6 pad.4.plan
  2.3 0.8 %reshape.30 = s32[128,16]{1,0:T(8,128)S(1)} reshape(s32[2048]{0:T(1024)} %param.11) | data formatting | bytes 16384 | tf_op jit(solution)/shard_map/reshape | solution.py:576
  3.1 0.7 copy.10
  3.8 69.3 %mhd_step.1 = (f32[8,128,512]{2,1,0:T(8,128)}, f32[8,512]{1,0:T(8,128)}) custom-call(f32[8,128,512]{2,1,0:T(8,128)} %state.1, f32[3,8,8,128]{3,2,1,0:T(8,128)} %jac.1, s32[32,128]{1,0:T(8,128)} %pad.4.plan, s32[16,128]{1,0:T(8,128)} %bitcast.4, s32[32,128]{1,0:T(8,128)} %bitcast.5, s32[32,128]{1,0:T(8,128)} %bitcast.6, f32[256,512]{1,0:T(8,128)} %conductance.1, ...), custom_call_target="tpu_custom_call" | custom-call | tf_op jit(solution)/shard_map/mhd_step/pallas_call | solution.py:582
  73.1 0.0 copy-start
  73.1 3.1 %copy.13 = f32[8,128,512]{2,1,0:T(8,128)} copy(f32[8,128,512]{2,1,0:T(8,128)} %get-tuple-element.4) | data formatting | bytes 4194304
  76.2 0.0 copy-done
  76.2 0.6 copy.14
Async XLA Ops:
  73.1 3.1 %copy-start = (f32[8,512]{1,0:T(8,128)S(1)}, f32[8,512]{1,0:T(8,128)}, u32[]{:S(2)}) copy-start(f32[8,512]{1,0:T(8,128)} %get-tuple-element.5) | copy-start | bytes 49156

commit v3 on v2

--- a/solution.py
+++ b/solution.py
@@ -12,6 +12,7 @@
 CAP = 70
 PEERS = 32
 SHELLS = 4
+EARLY = 8
 CFL_NUMBER = 0.3
 MESH = pl.DeviceIdType.MESH
 F32 = jnp.float32
@@ -55,7 +56,14 @@
     return y * 8 + z * 4 + x
 
 
-def column_plan(plan, cidx, copt, ccode):
+def column_plan(send, line, plan, cidx, copt, ccode):
+    slots = PEERS * CAP
+    line[:, 0:slots] = send[0:1, :] + 128 * send[1:2, :] + 512 * send[2:3, :] + 2048 * send[3:4, :]
+    line[:, slots:] = jnp.zeros((1, line.shape[1] - slots), jnp.int32)
+    for p in range(PEERS):
+        tile, shift = p * CAP // 128 * 128, p * CAP % 128
+        part = line[:, tile : tile + 256]
+        plan[p : p + 1, :] = (pltpu.roll(part, 256 - shift, 1) if shift else part)[:, 0:128]
     word = plan[...]
     row, level, quad = word & 511, (word >> 9) & 3, (word >> 11) & 3
     lane = iota(word.shape, 1)
@@ -75,7 +83,17 @@
 
 
 def column_targets(named, tgt):
-    value = named[...]
+    high, low = high_low(named[...].astype(F32))
+    both = jnp.concatenate([high, low, jnp.zeros((96, 128), F32)], axis=0).T.astype(BF16)
+    block = iota((128, 128), 1)
+    entry = iota((128, 128), 0)
+    widen = one_hot((entry & 15) * 8 <= block) * one_hot((entry & 15) * 8 + 8 > block) * one_hot(entry < 32)
+    wide = jnp.dot(both, widen, preferred_element_type=F32).reshape(8, 16, 128)
+    phase = iota((16, 128), 1) & 7
+    value = jnp.zeros((16, 128), F32)
+    for k in range(8):
+        value = jnp.where(phase == k, wide[k], value)
+    value = value.astype(jnp.int32)
     sender = (value * 59919) >> 22
     column = jnp.where(value < PEERS * CAP, value + sender * (128 - CAP), -1)
     for j in range(4):
@@ -156,7 +174,14 @@
     lax.fori_loop(0, 32, cell, 0)
 
 
-def add_ghosts(g, ghosts, jac, ws, change):
+def add_ghosts(g, ghosts, lower, upper, jac, ws, change):
+    for side, rim in enumerate((lower, upper)):
+        flux = jnp.zeros((64, 128), F32)
+        for h in range(8):
+            flux = flux + jac[0, pl.ds(g, 1), pl.ds(h, 1), :].reshape(1, 128) * rim[h]
+        spread = ws[0:1, :] * rim[pl.ds(g, 1)].reshape(64, 128)
+        part = (flux if side else -flux) - spread
+        change[pl.ds(g, 1), 7 * side] = change[pl.ds(g, 1), 7 * side] + part.reshape(1, 64, 128)
     for j in range(4):
         d = 1 + j // 2
         flux = jnp.zeros((8, 8, 128), F32)
@@ -228,11 +253,11 @@
 
 
 def whole_kernel(
-    state, jac, plan, named, vp, vc, conductance, lengths,
+    state, jac, send, named, vp, vc, conductance, lengths,
     new_state, thread_temp,
-    plain, u, lower, upper, table, mean, cidx, copt, ccode, tgt, slabs, recv, shell_max, own_max,
+    plain, u, lower, upper, table, mean, words, plan, cidx, copt, ccode, tgt, slabs, recv, noted, top, best_top, early_top, top_in,
     columns, acc, ghosts, change, ws, cells, picks, rows_of, weights, outgoing, arrived, back, returned,
-    state_sem, rim_send, rim_recv, shell_send, shell_recv, slab_send, slab_recv,
+    state_sem, rim_send, rim_recv, top_send, top_recv, early_send, early_recv, slab_send, slab_recv,
     out_send, out_recv, back_send, back_recv, local_sem, write_sem,
 ):
     me = lax.axis_index("blk")
@@ -259,57 +284,22 @@
 
     speed = jnp.max(jnp.sum(jnp.abs(jac[...]), axis=2), axis=1)
     ws[...] = speed
-    own_max[...] = jnp.broadcast_to(jnp.max(speed), (8, 128))
-    column_plan(plan, cidx, copt, ccode)
-    column_targets(named, tgt)
+    top[...] = jnp.broadcast_to(jnp.max(speed), (8, 128))
     u[:, :, 0:8, :] = jnp.zeros((8, 10, 8, 128), F32)
     u[:, :, 72:80, :] = jnp.zeros((8, 10, 8, 128), F32)
+    u[:, 0, 8:72, :] = jnp.zeros((8, 64, 128), F32)
+    u[:, 9, 8:72, :] = jnp.zeros((8, 64, 128), F32)
 
     for f in range(8):
         loads[f].wait()
         u[f, 1:9, 8:72, :] = plain[f].T.reshape(8, 64, 128)
 
-    pl.semaphore_wait(barrier, PEERS + SHELLS - 2)
-
-    def shell_copy(d):
-        return pltpu.make_async_remote_copy(
-            src_ref=own_max, dst_ref=shell_max.at[d], send_sem=shell_send.at[d],
-            recv_sem=shell_recv.at[d],
-            device_id={"shell": lax.rem(shell + d, SHELLS)}, device_id_type=MESH,
-        )
-
-    for d in range(1, SHELLS):
-        shell_copy(d).start()
-
-    def rim_up():
-        return pltpu.make_async_remote_copy(
-            src_ref=u.at[:, 8, 8:72], dst_ref=lower, send_sem=rim_send.at[0], recv_sem=rim_recv.at[0],
-            device_id={"shell": lax.rem(shell + 1, SHELLS)}, device_id_type=MESH,
-        )
-
-    def rim_down():
-        return pltpu.make_async_remote_copy(
-            src_ref=u.at[:, 1, 8:72], dst_ref=upper, send_sem=rim_send.at[1], recv_sem=rim_recv.at[1],
-            device_id={"shell": lax.rem(shell + SHELLS - 1, SHELLS)}, device_id_type=MESH,
-        )
-
-    @pl.when(shell < SHELLS - 1)
-    def _():
-        rim_up().start()
-
-    @pl.when(shell > 0)
-    def _():
-        rim_down().start()
-
     build_table(u, table, mean)
+    column_plan(send, words, plan, cidx, copt, ccode)
     points = jnp.concatenate([vp[pl.ds(c, 8, stride=4), :] for c in range(4)], axis=1)
     used = points < 256 * 512
     owner = jnp.max(jnp.where(used, points >> 12, -1), axis=1, keepdims=True)
     local = jnp.where(used, points & 4095, -1).astype(F32) + 1.0
-    best = own_max[...]
-    for d in range(1, SHELLS):
-        shell_copy(d).wait()
-        best = jnp.maximum(best, shell_max[d])
 
     def slab_copy(n, sign):
         peer = partner(me, n, 1)
@@ -320,7 +310,7 @@
             device_id={"blk": peer}, device_id_type=MESH,
         )
 
-    def pack(i, carry):
+    def pack(i, best, send):
         pair = [partner(me, 2 * i, 1), partner(me, 2 * i + 1, 1)]
         index = jnp.concatenate([cidx[pl.ds(p, 1), :] for p in pair], axis=1)
         option = jnp.concatenate([copt[pl.ds(p, 1), :] for p in pair], axis=1)
@@ -333,42 +323,90 @@
             )
         for half in range(2):
             peer = pair[half]
-            slabs[peer, 0:128, :] = chosen[:, half * 128 : half * 128 + 128]
             run = jnp.sum(jnp.where(owner == peer, local, 0.0), axis=0, keepdims=True) - 1.0
-            rows = [ccode[pl.ds(peer, 1), :]] + lanes_to_rows(run) + [best[0:1, :], jnp.zeros((2, 128), F32)]
-            slabs[peer, 128:136, :] = jnp.concatenate(rows, axis=0)
-            if half == 0:
-
-                @pl.when(i > 0)
-                def _():
-                    slab_copy(2 * i, 1).start()
-
-            else:
-                slab_copy(2 * i + 1, 1).start()
-        return carry
-
-    lax.fori_loop(0, PEERS // 2, pack, 0)
-    recv[me] = slabs[me]
+            none = jnp.zeros((1, 128), F32)
+            rows = [none, ccode[pl.ds(peer, 1), :]] + lanes_to_rows(run) + [best, none]
+            notes = jnp.concatenate([jnp.zeros((120, 128), F32)] + rows, axis=0).T
+            piece = chosen[:, half * 128 : half * 128 + 128]
+            slabs[peer] = jnp.where(iota((128, 128), 1) > 120, notes, piece)
+            if send:
+                slab_copy(2 * i + half, 1).start()
+
+    def pack_first(i, carry):
+        pack(i, carry, False)
+        return carry
+
+    def pack_rest(i, carry):
+        pack(i, carry, True)
+        return carry
+
+    lax.fori_loop(0, EARLY // 2, pack_first, top[0:1, :])
+    pl.semaphore_wait(barrier, PEERS + SHELLS - 2)
+
+    def top_copy(d):
+        return pltpu.make_async_remote_copy(
+            src_ref=top, dst_ref=top_in.at[d], send_sem=top_send.at[d], recv_sem=top_recv.at[d],
+            device_id={"shell": lax.rem(shell + d, SHELLS)}, device_id_type=MESH,
+        )
+
+    for d in range(1, SHELLS):
+        top_copy(d).start()
+
+    def rim_up():
+        return pltpu.make_async_remote_copy(
+            src_ref=u.at[:, 8, 8:72], dst_ref=lower, send_sem=rim_send.at[0], recv_sem=rim_recv.at[0],
+            device_id={"shell": lax.rem(shell + 1, SHELLS)}, device_id_type=MESH,
+        )
+
+    def rim_down():
+        return pltpu.make_async_remote_copy(
+            src_ref=u.at[:, 1, 8:72], dst_ref=upper, send_sem=rim_send.at[1], recv_sem=rim_recv.at[1],
+            device_id={"shell": lax.rem(shell + SHELLS - 1, SHELLS)}, device_id_type=MESH,
+        )
+
+    @pl.when(shell < SHELLS - 1)
+    def _():
+        rim_up().start()
 
     @pl.when(shell > 0)
     def _():
-        rim_up().wait_recv()
-        u[:, 0, 8:72, :] = lower[...]
+        rim_down().start()
+
+    def send_early(n, carry):
+        slab_copy(n, 1).start()
+        return carry
+
+    lax.fori_loop(1, EARLY, send_early, 0)
+    best = top[0:1, :]
+    for d in range(1, SHELLS):
+        top_copy(d).wait()
+        best = jnp.maximum(best, top_in[d, 0:1, :])
+    best_top[...] = jnp.broadcast_to(best, (8, 128))
+
+    def early_copy(n):
+        return pltpu.make_async_remote_copy(
+            src_ref=best_top, dst_ref=early_top.at[n], send_sem=early_send.at[n], recv_sem=early_recv.at[n],
+            device_id={"blk": partner(me, n, 1)}, device_id_type=MESH,
+        )
+
+    def send_top(n, carry):
+        early_copy(n).start()
+        return carry
+
+    lax.fori_loop(1, EARLY, send_top, 0)
+    lax.fori_loop(EARLY // 2, PEERS // 2, pack_rest, best)
+    recv[me] = slabs[me]
 
     @pl.when(shell == 0)
     def _():
-        u[:, 0, 8:72, :] = u[:, 1, 8:72, :]
-
-    @pl.when(shell < SHELLS - 1)
-    def _():
-        rim_down().wait_recv()
-        u[:, 9, 8:72, :] = upper[...]
+        lower[...] = u[:, 1, 8:72, :]
 
     @pl.when(shell == SHELLS - 1)
     def _():
-        u[:, 9, 8:72, :] = u[:, 8, 8:72, :]
+        upper[...] = u[:, 8, 8:72, :]
 
     inner_step(u, jac, ws, change)
+    column_targets(named, tgt)
 
     def columns_of(n, carry):
         wanted = tgt[...] - partner(me, n, -1) * 128
@@ -380,7 +418,7 @@
     for run in range(8):
         cells[run] = one_hot(iota((512, 512), 0) == (where_to[run : run + 1, :] & 511))
 
-    def arrive(i, top):
+    def arrive(i, fastest):
         tiles = []
         for k in range(4):
             n = 4 * i + k
@@ -392,12 +430,15 @@
 
             else:
                 slab_copy(n, -1).wait()
-            slab = recv[partner(me, n, -1)]
-            high, low = high_low(slab[0:128])
+            sender = partner(me, n, -1)
+            slab = recv[sender]
+            note = slab.T[120:128]
+            noted[sender] = note
+            fastest = jnp.maximum(fastest, note[6:7])
+            high, low = high_low(slab)
             tiles.append(
-                jnp.concatenate([low, high, slab[128:136], jnp.zeros((8, 128), F32)], axis=0).astype(BF16)
+                jnp.concatenate([low, high, jnp.broadcast_to(note[1:2], (16, 128))], axis=0).astype(BF16)
             )
-            top = jnp.maximum(top, slab[133:134])
         rows = jnp.concatenate(tiles, axis=1)
         for n in range(4):
             lanes = slice(n * 512, (n + 1) * 512)
@@ -405,14 +446,29 @@
                 rows, columns[pl.ds(pl.multiple_of(i * 512, 512), 512), lanes], preferred_element_type=F32
             )
             acc[:, lanes] = acc[:, lanes] + part
-        return top
+        return fastest
 
     acc[...] = jnp.zeros_like(acc)
-    top = lax.fori_loop(0, PEERS // 4, arrive, jnp.zeros((1, 128), F32))
+    fastest = lax.fori_loop(0, PEERS // 4, arrive, best)
+
+    def get_top(n, carry):
+        early_copy(n).wait()
+        return jnp.maximum(carry, early_top[n, 0:1, :])
+
+    fastest = lax.fori_loop(1, EARLY, get_top, fastest)
+
+    @pl.when(shell > 0)
+    def _():
+        rim_up().wait_recv()
+
+    @pl.when(shell < SHELLS - 1)
+    def _():
+        rim_down().wait_recv()
+
     ghost_layers(acc, ghosts, spread=mean)
-    ratio = (0.5 * (CFL_NUMBER / top)).reshape(1, 1, 1, 128)
-
-    add_ghosts(7, ghosts, jac, ws, change)
+    ratio = (0.5 * (CFL_NUMBER / fastest)).reshape(1, 1, 1, 128)
+
+    add_ghosts(7, ghosts, lower, upper, jac, ws, change)
     advance_field(7, u, change, ratio, plain)
     high, low = high_low(plain[7])
     rows = jnp.concatenate([high, low], axis=0).astype(BF16)
@@ -448,7 +504,7 @@
         for k in range(4):
             lanes = slice(k * 512, (k + 1) * 512)
             s = partner(me, 4 * i + k, -1)
-            point = jnp.concatenate([recv[s, 129 + c : 130 + c, :] for c in range(4)], axis=1).astype(jnp.int32)
+            point = jnp.concatenate([noted[s, 2 + c : 3 + c, :] for c in range(4)], axis=1).astype(jnp.int32)
             picks[i, :, lanes] = one_hot(iota((128, 512), 0) == (point & 127))
             row = ((point >> 7) & 3) * 8 + (point >> 9)
             rows_of[i, :, lanes] = jnp.broadcast_to(jnp.where(point < 0, -1, row), (8, 512))
@@ -459,7 +515,7 @@
     writes = [pltpu.make_async_copy(plain.at[f], new_state.at[f], write_sem.at[f]) for f in range(8)]
 
     def other_field(g, carry):
-        add_ghosts(g, ghosts, jac, ws, change)
+        add_ghosts(g, ghosts, lower, upper, jac, ws, change)
         advance_field(g, u, change, ratio, plain)
         return carry
 
@@ -467,30 +523,21 @@
     for f in range(3):
         writes[f].start()
 
-    def collect(i, total):
-        parts = []
-        for k in range(4):
-            n = 4 * i + k
-            s = partner(me, n, -1)
-            if k == 0:
-
-                @pl.when(i > 0)
-                def _():
-                    line_copy(outgoing, arrived, n, -1, out_send, out_recv).wait()
-
-            else:
-                line_copy(outgoing, arrived, n, -1, out_send, out_recv).wait()
-            high, low = high_low(rows_to_lanes(arrived, s))
-            mask = iota((32, 512), 0) == rows_of[i, 0:1, k * 512 : (k + 1) * 512]
-            parts.append(
-                jnp.concatenate([jnp.where(mask, high, 0.0), jnp.where(mask, low, 0.0)], axis=0).astype(BF16)
-            )
-        return total + lax.dot_general(
-            jnp.concatenate(parts, axis=1), picks[i], (((1,), (1,)), ((), ())), preferred_element_type=F32
-        )
-
-    total = lax.fori_loop(0, PEERS // 4, collect, jnp.zeros((64, 128), F32))
-    total = total[0:32] + total[32:64]
+    def get_out(n, carry):
+        line_copy(outgoing, arrived, n, -1, out_send, out_recv).wait()
+        return carry
+
+    lax.fori_loop(1, PEERS, get_out, 0)
+    total = jnp.zeros((128, 64), F32)
+    for i in range(PEERS // 4):
+        mask = one_hot(iota((32, 2048), 0) == rows_of[i, 0:1, :])
+        line = jnp.concatenate([rows_to_lanes(arrived, partner(me, 4 * i + k, -1)) for k in range(4)], axis=1)
+        high, low = high_low(line)
+        rows = jnp.concatenate([mask * high.astype(BF16), mask * low.astype(BF16)], axis=0)
+        total = total + lax.dot_general(
+            picks[i], rows, (((1,), (1,)), ((), ())), preferred_element_type=F32
+        )
+    total = (total[:, 0:32] + total[:, 32:64]).T
     rhs = jnp.concatenate([total[c * 8 : (c + 1) * 8] for c in range(4)], axis=1)
     first = me * 8
     here = iota((8, 128), 1) == lax.rem(first, 128) + iota((8, 128), 0)
@@ -502,18 +549,14 @@
     high, low = high_low(solved)
     answers = jnp.concatenate(lanes_to_rows(high) + lanes_to_rows(low), axis=0).astype(BF16)
 
-    def answer(i, carry):
+    for i in range(PEERS // 4):
         got = jnp.dot(answers, picks[i], preferred_element_type=F32)
         got = got[0:32] + got[32:64]
         mask = iota((32, 2048), 0) == rows_of[i, 0:1, :]
         line = jnp.sum(jnp.where(mask, got, 0.0), axis=0, keepdims=True)
         for k in range(4):
-            n = 4 * i + k
             part = lanes_to_rows(line[:, k * 512 : (k + 1) * 512])
-            back[partner(me, n, -1)] = jnp.concatenate(part + [jnp.zeros((4, 128), F32)], axis=0)
-        return carry
-
-    lax.fori_loop(0, PEERS // 4, answer, 0)
+            back[partner(me, 4 * i + k, -1)] = jnp.concatenate(part + [jnp.zeros((4, 128), F32)], axis=0)
 
     def send_back(n, carry):
         line_copy(back, returned, n, 1, back_send, back_recv).start()
@@ -566,18 +609,28 @@
         rim_down().wait_send()
 
 
+def hand_over(state, temp, new_state, thread_temp, buffer, small, sem, out_sem):
+    loads = [pltpu.make_async_copy(state.at[f], buffer.at[f], sem.at[f]) for f in range(8)]
+    loads.append(pltpu.make_async_copy(temp, small, sem.at[8]))
+    stores = [pltpu.make_async_copy(buffer.at[f], new_state.at[f], out_sem.at[f]) for f in range(8)]
+    stores.append(pltpu.make_async_copy(small, thread_temp, out_sem.at[8]))
+    for load in loads:
+        load.start()
+    for load, store in zip(loads, stores):
+        load.wait()
+        store.start()
+    for store in stores:
+        store.wait()
+
+
 def on_device(
     plasma_state, jacobian, send_list, recv_map, visit_point, visit_cell, conductance, lengths
 ):
     fields, blocks, cells = plasma_state.shape
-    block, face, level, quad = send_list[0], send_list[1], send_list[2], send_list[3]
-    plan = (block + 128 * face + 512 * level + 2048 * quad).reshape(PEERS, CAP)
-    plan = jnp.pad(plan, ((0, 0), (0, 128 - CAP)))
-    named = recv_map.reshape(blocks, 16).T
     shape = jax.ShapeDtypeStruct
     vmem = pl.BlockSpec(memory_space=pltpu.VMEM)
     anywhere = pl.BlockSpec(memory_space=pl.ANY)
-    dma = lambda n: pltpu.SemaphoreType.DMA((n,))
+    dma = lambda *dims: pltpu.SemaphoreType.DMA(dims)
     buffer = lambda *dims: pltpu.VMEM(dims, F32)
     new_state, thread_temp = pl.pallas_call(
         whole_kernel,
@@ -591,14 +644,19 @@
             buffer(fields, 64, 128),
             pltpu.VMEM((1280, 512), BF16),
             buffer(256, 128),
+            pltpu.VMEM((1, 2432), jnp.int32),
+            pltpu.VMEM((PEERS, 128), jnp.int32),
             pltpu.VMEM((PEERS, 128), jnp.int32),
             pltpu.VMEM((PEERS, 128), jnp.int32),
             buffer(PEERS, 128),
             pltpu.VMEM((1, 2048), jnp.int32),
-            buffer(PEERS, 136, 128),
-            buffer(PEERS, 136, 128),
+            buffer(PEERS, 128, 128),
+            buffer(PEERS, 128, 128),
+            buffer(PEERS, 8, 128),
+            buffer(8, 128),
+            buffer(8, 128),
+            buffer(8, 8, 128),
             buffer(SHELLS, 8, 128),
-            buffer(8, 128),
             pltpu.VMEM((PEERS * 128, 2048), BF16),
             buffer(272, 2048),
             buffer(4, fields, 8, 8, 128),
@@ -612,7 +670,7 @@
             buffer(PEERS, 8, 128),
             buffer(PEERS, 8, 128),
             buffer(PEERS, 8, 128),
-            dma(8), dma(2), dma(2), dma(SHELLS), dma(SHELLS), dma(PEERS), dma(PEERS),
+            dma(8), dma(2), dma(2), dma(SHELLS), dma(SHELLS), dma(8), dma(8), dma(PEERS), dma(PEERS),
             dma(PEERS), dma(PEERS), dma(PEERS), dma(PEERS), dma(1), dma(8),
         ],
         compiler_params=pltpu.CompilerParams(
@@ -620,10 +678,18 @@
         ),
         name="mhd_step",
     )(
-        plasma_state, jacobian, plan, named, visit_point.reshape(-1, 128), visit_cell.reshape(-1, 128),
+        plasma_state, jacobian, send_list, recv_map.reshape(-1, 128), visit_point.reshape(-1, 128), visit_cell.reshape(-1, 128),
         conductance, lengths.reshape(-1, 128),
     )
-    return (new_state, thread_temp)
+    return pl.pallas_call(
+        hand_over,
+        in_specs=[anywhere, anywhere],
+        out_specs=[anywhere, anywhere],
+        out_shape=[shape((fields, blocks, cells), F32), shape((8, 512), F32)],
+        scratch_shapes=[buffer(fields, blocks, cells), buffer(8, 512), dma(fields + 1), dma(fields + 1)],
+        compiler_params=pltpu.CompilerParams(vmem_limit_bytes=VMEM_BYTES),
+        name="hand_over",
+    )(new_state, thread_temp)
 
 
 def solution(mesh):

time: 77.1 us -> 72.5 us (0.940)
  local copies, waits for them, and re-layouts: 5.85 us -> 0 us
  Pallas kernels: 69.3 us -> 71.3 us
  other arithmetic: 0.99 us -> 0 us
    unnamed x4 -> x0, local copies, waits for them, and re-layouts: 3.69 us -> none
    pallas_call x0 -> x1, Pallas kernels: none -> 2.41 us  [on_device(): pl.pallas_call(hand_over, in_specs=[anywhere, anywhere], out_specs=[anywh...]
    reshape x2 -> x0, local copies, waits for them, and re-layouts: 1.44 us -> none  [on_device(): named = recv_map.reshape(blocks, 16).T]
    add x1 -> x0, other arithmetic: 0.99 us -> none  [on_device(): plan = (block + 128 * face + 512 * level + 2048 * quad).reshape(PEERS, CAP)]
where the time goes in v3:
time: 72.5 us; the launch traced here: 72.1 us
  Pallas kernels  71.3 us (98%)
  between operations  0.8 us (1%)
    pallas_call x1, Pallas kernels, on_device(): pl.pallas_call(whole_kernel, in_specs=[anywhere, vmem, vmem, vmem, vmem,...  68.9 us
    pallas_call x1, Pallas kernels, on_device(): pl.pallas_call(hand_over, in_specs=[anywhere, anywhere], out_specs=[anywh...  2.41 us

profile of v3, /device:TPU:0, one launch (start us, length us, event | category | flops | bytes accessed | tf_op | source)
XLA Modules:
  0.0 72.1 jit_solution(5516125071101890954)
XLA Ops:
  0.6 68.9 %mhd_step.1 = (f32[8,128,512]{2,1,0:T(8,128)}, f32[8,512]{1,0:T(8,128)}) custom-call(f32[8,128,512]{2,1,0:T(8,128)} %state.1, f32[3,8,8,128]{3,2,1,0:T(8,128)} %jac.1, s32[4,2240]{1,0:T(4,128)} %send.1, s32[16,128]{1,0:T(8,128)} %bitcast.6, s32[32,128]{1,0:T(8,128)} %bitcast.4, s32[32,128]{1,0:T(8,128)} %bitcast.5, f32[256,512]{1,0:T(8,128)} %conductance.1, ...), custom_call_target="tpu_custom_call" | custom-call | tf_op jit(solution)/shard_map/mhd_step/pallas_call | solution.py:635
  69.5 2.4 %hand_over.1 = (f32[8,128,512]{2,1,0:T(8,128)}, f32[8,512]{1,0:T(8,128)}) custom-call(f32[8,128,512]{2,1,0:T(8,128)} %get-tuple-element.4.state, f32[8,512]{1,0:T(8,128)} %get-tuple-element.5.temp), custom_call_target="tpu_custom_call" | custom-call | tf_op jit(solution)/shard_map/hand_over/pallas_call | solution.py:684

commit v4 on v3

--- a/solution.py
+++ b/solution.py
@@ -17,7 +17,7 @@
 MESH = pl.DeviceIdType.MESH
 F32 = jnp.float32
 BF16 = jnp.bfloat16
-VMEM_BYTES = 60 * 1024 * 1024
+VMEM_BYTES = 63000 * 1024
 
 
 def iota(shape, dim):
@@ -47,7 +47,7 @@
 
 
 def partner(me, n, sign):
-    offset = lax.rem(11 * n, PEERS)
+    offset = lax.rem(3 * n, PEERS)
     dy, dz, dx = lax.div(offset, 8), lax.rem(lax.div(offset, 4), 2), lax.rem(offset, 4)
     y, z, x = lax.div(me, 8), lax.rem(lax.div(me, 4), 2), lax.rem(me, 4)
     y = lax.rem(y + 4 + sign * dy, 4)
@@ -253,35 +253,38 @@
 
 
 def whole_kernel(
-    state, jac, send, named, vp, vc, conductance, lengths,
-    new_state, thread_temp,
-    plain, u, lower, upper, table, mean, words, plan, cidx, copt, ccode, tgt, slabs, recv, noted, top, best_top, early_top, top_in,
-    columns, acc, ghosts, change, ws, cells, picks, rows_of, weights, outgoing, arrived, back, returned,
+    state, jac_in, send_in, named_in, vp_in, vc_in, conductance, lengths_in,
+    plain, thread_temp,
+    jac, send, named, vp, vc, lengths, u, lower, upper, table, mean, words, plan, cidx, copt, ccode, tgt, slabs, recv, noted, top, best_top, early_top, top_in,
+    acc, ghosts, change, ws, cells, picks, rows_of, weights, outgoing, arrived, back, returned,
     state_sem, rim_send, rim_recv, top_send, top_recv, early_send, early_recv, slab_send, slab_recv,
-    out_send, out_recv, back_send, back_recv, local_sem, write_sem,
+    out_send, out_recv, back_send, back_recv, local_sem,
 ):
     me = lax.axis_index("blk")
     shell = lax.axis_index("shell")
     barrier = pltpu.get_barrier_semaphore()
 
+    def greet(n, carry):
+        pl.semaphore_signal(barrier, inc=1, device_id={"blk": partner(me, n, 1)}, device_id_type=MESH)
+        return carry
+
+    lax.fori_loop(1, PEERS, greet, 0)
+    for d in range(1, SHELLS):
+        pl.semaphore_signal(
+            barrier, inc=1, device_id={"shell": lax.rem(shell + d, SHELLS)}, device_id_type=MESH
+        )
+
     loads = [pltpu.make_async_copy(state.at[f], plain.at[f], state_sem.at[f]) for f in range(8)]
-    for load in loads:
+    pairs = ((jac_in, jac), (send_in, send), (vp_in, vp), (named_in, named), (vc_in, vc), (lengths_in, lengths))
+    small = [pltpu.make_async_copy(src, dst, local_sem.at[1 + i]) for i, (src, dst) in enumerate(pairs)]
+    for load in small + loads:
         load.start()
     weight_load = pltpu.make_async_copy(
         conductance.at[pl.ds(pl.multiple_of(me * 8, 8), 8)], weights, local_sem.at[0]
     )
     weight_load.start()
 
-    def greet(n, carry):
-        pl.semaphore_signal(barrier, inc=1, device_id={"blk": partner(me, n, 1)}, device_id_type=MESH)
-        return carry
-
-    lax.fori_loop(1, PEERS, greet, 0)
-    for d in range(1, SHELLS):
-        pl.semaphore_signal(
-            barrier, inc=1, device_id={"shell": lax.rem(shell + d, SHELLS)}, device_id_type=MESH
-        )
-
+    small[0].wait()
     speed = jnp.max(jnp.sum(jnp.abs(jac[...]), axis=2), axis=1)
     ws[...] = speed
     top[...] = jnp.broadcast_to(jnp.max(speed), (8, 128))
@@ -295,19 +298,19 @@
         u[f, 1:9, 8:72, :] = plain[f].T.reshape(8, 64, 128)
 
     build_table(u, table, mean)
+    for load in small[1:]:
+        load.wait()
     column_plan(send, words, plan, cidx, copt, ccode)
     points = jnp.concatenate([vp[pl.ds(c, 8, stride=4), :] for c in range(4)], axis=1)
     used = points < 256 * 512
     owner = jnp.max(jnp.where(used, points >> 12, -1), axis=1, keepdims=True)
     local = jnp.where(used, points & 4095, -1).astype(F32) + 1.0
 
-    def slab_copy(n, sign):
-        peer = partner(me, n, 1)
-        slot = me if sign > 0 else partner(me, n, -1)
+    def slab_copy(n):
         return pltpu.make_async_remote_copy(
-            src_ref=slabs.at[peer], dst_ref=recv.at[slot],
+            src_ref=slabs.at[n], dst_ref=recv.at[n],
             send_sem=slab_send.at[n], recv_sem=slab_recv.at[n],
-            device_id={"blk": peer}, device_id_type=MESH,
+            device_id={"blk": partner(me, n, 1)}, device_id_type=MESH,
         )
 
     def pack(i, best, send):
@@ -328,9 +331,9 @@
             rows = [none, ccode[pl.ds(peer, 1), :]] + lanes_to_rows(run) + [best, none]
             notes = jnp.concatenate([jnp.zeros((120, 128), F32)] + rows, axis=0).T
             piece = chosen[:, half * 128 : half * 128 + 128]
-            slabs[peer] = jnp.where(iota((128, 128), 1) > 120, notes, piece)
+            slabs[2 * i + half] = jnp.where(iota((128, 128), 1) > 120, notes, piece)
             if send:
-                slab_copy(2 * i + half, 1).start()
+                slab_copy(2 * i + half).start()
 
     def pack_first(i, carry):
         pack(i, carry, False)
@@ -373,7 +376,7 @@
         rim_down().start()
 
     def send_early(n, carry):
-        slab_copy(n, 1).start()
+        slab_copy(n).start()
         return carry
 
     lax.fori_loop(1, EARLY, send_early, 0)
@@ -395,7 +398,7 @@
 
     lax.fori_loop(1, EARLY, send_top, 0)
     lax.fori_loop(EARLY // 2, PEERS // 2, pack_rest, best)
-    recv[me] = slabs[me]
+    recv[0] = slabs[0]
 
     @pl.when(shell == 0)
     def _():
@@ -408,12 +411,6 @@
     inner_step(u, jac, ws, change)
     column_targets(named, tgt)
 
-    def columns_of(n, carry):
-        wanted = tgt[...] - partner(me, n, -1) * 128
-        columns[pl.ds(pl.multiple_of(n * 128, 128), 128), :] = one_hot(iota((128, 2048), 0) == wanted)
-        return carry
-
-    lax.fori_loop(0, PEERS, columns_of, 0)
     where_to = jnp.concatenate([vc[pl.ds(c, 8, stride=4), :] for c in range(4)], axis=1)
     for run in range(8):
         cells[run] = one_hot(iota((512, 512), 0) == (where_to[run : run + 1, :] & 511))
@@ -426,25 +423,25 @@
 
                 @pl.when(i > 0)
                 def _():
-                    slab_copy(n, -1).wait()
+                    slab_copy(n).wait()
 
             else:
-                slab_copy(n, -1).wait()
-            sender = partner(me, n, -1)
-            slab = recv[sender]
+                slab_copy(n).wait()
+            slab = recv[n]
             note = slab.T[120:128]
-            noted[sender] = note
+            noted[n] = note
             fastest = jnp.maximum(fastest, note[6:7])
             high, low = high_low(slab)
             tiles.append(
                 jnp.concatenate([low, high, jnp.broadcast_to(note[1:2], (16, 128))], axis=0).astype(BF16)
             )
         rows = jnp.concatenate(tiles, axis=1)
+        starts = [partner(me, 4 * i + k, -1) * 128 for k in range(4)]
         for n in range(4):
             lanes = slice(n * 512, (n + 1) * 512)
-            part = jnp.dot(
-                rows, columns[pl.ds(pl.multiple_of(i * 512, 512), 512), lanes], preferred_element_type=F32
-            )
+            wanted = tgt[:, lanes]
+            picked = [one_hot(iota((128, 512), 0) == wanted - start) for start in starts]
+            part = jnp.dot(rows, jnp.concatenate(picked, axis=0), preferred_element_type=F32)
             acc[:, lanes] = acc[:, lanes] + part
         return fastest
 
@@ -485,25 +482,30 @@
     for c in range(4):
         outgoing[:, c, :] = total[:, c * 128 : (c + 1) * 128]
 
-    def line_copy(src, dst, n, sign, ssem, rsem):
+    def out_copy(n):
         peer = partner(me, n, 1)
-        slot = me if sign > 0 else partner(me, n, -1)
         return pltpu.make_async_remote_copy(
-            src_ref=src.at[peer], dst_ref=dst.at[slot], send_sem=ssem.at[n], recv_sem=rsem.at[n],
+            src_ref=outgoing.at[peer], dst_ref=arrived.at[n], send_sem=out_send.at[n], recv_sem=out_recv.at[n],
             device_id={"blk": peer}, device_id_type=MESH,
         )
 
+    def back_copy(n):
+        return pltpu.make_async_remote_copy(
+            src_ref=back.at[n], dst_ref=returned.at[n], send_sem=back_send.at[n], recv_sem=back_recv.at[n],
+            device_id={"blk": partner(me, n, -1)}, device_id_type=MESH,
+        )
+
     def send_out(n, carry):
-        line_copy(outgoing, arrived, n, 1, out_send, out_recv).start()
+        out_copy(n).start()
         return carry
 
     lax.fori_loop(1, PEERS, send_out, 0)
-    arrived[me] = outgoing[me]
+    arrived[0] = outgoing[me]
 
     def prepare(i, carry):
         for k in range(4):
             lanes = slice(k * 512, (k + 1) * 512)
-            s = partner(me, 4 * i + k, -1)
+            s = 4 * i + k
             point = jnp.concatenate([noted[s, 2 + c : 3 + c, :] for c in range(4)], axis=1).astype(jnp.int32)
             picks[i, :, lanes] = one_hot(iota((128, 512), 0) == (point & 127))
             row = ((point >> 7) & 3) * 8 + (point >> 9)
@@ -512,7 +514,6 @@
 
     lax.fori_loop(0, PEERS // 4, prepare, 0)
 
-    writes = [pltpu.make_async_copy(plain.at[f], new_state.at[f], write_sem.at[f]) for f in range(8)]
 
     def other_field(g, carry):
         add_ghosts(g, ghosts, lower, upper, jac, ws, change)
@@ -520,18 +521,16 @@
         return carry
 
     lax.fori_loop(0, 3, other_field, 0)
-    for f in range(3):
-        writes[f].start()
 
     def get_out(n, carry):
-        line_copy(outgoing, arrived, n, -1, out_send, out_recv).wait()
+        out_copy(n).wait()
         return carry
 
     lax.fori_loop(1, PEERS, get_out, 0)
     total = jnp.zeros((128, 64), F32)
     for i in range(PEERS // 4):
         mask = one_hot(iota((32, 2048), 0) == rows_of[i, 0:1, :])
-        line = jnp.concatenate([rows_to_lanes(arrived, partner(me, 4 * i + k, -1)) for k in range(4)], axis=1)
+        line = jnp.concatenate([rows_to_lanes(arrived, 4 * i + k) for k in range(4)], axis=1)
         high, low = high_low(line)
         rows = jnp.concatenate([mask * high.astype(BF16), mask * low.astype(BF16)], axis=0)
         total = total + lax.dot_general(
@@ -556,18 +555,16 @@
         line = jnp.sum(jnp.where(mask, got, 0.0), axis=0, keepdims=True)
         for k in range(4):
             part = lanes_to_rows(line[:, k * 512 : (k + 1) * 512])
-            back[partner(me, 4 * i + k, -1)] = jnp.concatenate(part + [jnp.zeros((4, 128), F32)], axis=0)
+            back[4 * i + k] = jnp.concatenate(part + [jnp.zeros((4, 128), F32)], axis=0)
 
     def send_back(n, carry):
-        line_copy(back, returned, n, 1, back_send, back_recv).start()
+        back_copy(n).start()
         return carry
 
     lax.fori_loop(1, PEERS, send_back, 0)
-    returned[me] = back[me]
+    returned[0] = back[0]
 
     lax.fori_loop(3, 7, other_field, 0)
-    for f in range(3, 7):
-        writes[f].start()
 
     visited = jnp.where(used, block, -1)
     cover = jnp.zeros((128, 512), F32)
@@ -578,13 +575,13 @@
         )
 
     def get_back(n, carry):
-        line_copy(back, returned, n, -1, back_send, back_recv).wait()
+        back_copy(n).wait()
         return carry
 
     lax.fori_loop(1, PEERS, get_back, 0)
     values = jnp.zeros((8, 512), F32)
-    for o in range(PEERS):
-        values = jnp.where(owner == o, rows_to_lanes(returned, o), values)
+    for n in range(PEERS):
+        values = jnp.where(owner == partner(me, n, 1), rows_to_lanes(returned, n), values)
     high, low = high_low(values)
     total = jnp.zeros((256, 512), F32)
     for run in range(8):
@@ -596,9 +593,6 @@
             rows, cells[run], (((1,), (1,)), ((), ())), preferred_element_type=F32
         )
     plain[7] = jnp.where(cover > 0.5, total[0:128] + total[128:256], plain[7])
-    writes[7].start()
-    for write in writes:
-        write.wait()
 
     @pl.when(shell < SHELLS - 1)
     def _():
@@ -609,18 +603,15 @@
         rim_down().wait_send()
 
 
-def hand_over(state, temp, new_state, thread_temp, buffer, small, sem, out_sem):
-    loads = [pltpu.make_async_copy(state.at[f], buffer.at[f], sem.at[f]) for f in range(8)]
-    loads.append(pltpu.make_async_copy(temp, small, sem.at[8]))
-    stores = [pltpu.make_async_copy(buffer.at[f], new_state.at[f], out_sem.at[f]) for f in range(8)]
-    stores.append(pltpu.make_async_copy(small, thread_temp, out_sem.at[8]))
-    for load in loads:
-        load.start()
-    for load, store in zip(loads, stores):
-        load.wait()
-        store.start()
-    for store in stores:
-        store.wait()
+def hand_over(state, temp, new_state, thread_temp, sem):
+    copies = [
+        pltpu.make_async_copy(state, new_state, sem.at[0]),
+        pltpu.make_async_copy(temp, thread_temp, sem.at[1]),
+    ]
+    for copy in copies:
+        copy.start()
+    for copy in copies:
+        copy.wait()
 
 
 def on_device(
@@ -634,11 +625,16 @@
     buffer = lambda *dims: pltpu.VMEM(dims, F32)
     new_state, thread_temp = pl.pallas_call(
         whole_kernel,
-        in_specs=[anywhere, vmem, vmem, vmem, vmem, vmem, anywhere, vmem],
-        out_specs=[anywhere, vmem],
-        out_shape=[shape((fields, blocks, cells), F32), shape((8, 512), F32)],
+        in_specs=[pl.BlockSpec(memory_space=pltpu.HBM)] * 8,
+        out_specs=[vmem, vmem],
+        out_shape=[pltpu.VMEM((fields, blocks, cells), F32), pltpu.VMEM((8, 512), F32)],
         scratch_shapes=[
-            buffer(fields, blocks, cells),
+            buffer(3, fields, fields, blocks),
+            pltpu.VMEM(send_list.shape, jnp.int32),
+            pltpu.VMEM((16, 128), jnp.int32),
+            pltpu.VMEM((32, 128), jnp.int32),
+            pltpu.VMEM((32, 128), jnp.int32),
+            pltpu.VMEM((2, 128), jnp.int32),
             buffer(fields, 10, 80, 128),
             buffer(fields, 64, 128),
             buffer(fields, 64, 128),
@@ -657,7 +653,6 @@
             buffer(8, 128),
             buffer(8, 8, 128),
             buffer(SHELLS, 8, 128),
-            pltpu.VMEM((PEERS * 128, 2048), BF16),
             buffer(272, 2048),
             buffer(4, fields, 8, 8, 128),
             buffer(fields, 8, 64, 128),
@@ -671,7 +666,7 @@
             buffer(PEERS, 8, 128),
             buffer(PEERS, 8, 128),
             dma(8), dma(2), dma(2), dma(SHELLS), dma(SHELLS), dma(8), dma(8), dma(PEERS), dma(PEERS),
-            dma(PEERS), dma(PEERS), dma(PEERS), dma(PEERS), dma(1), dma(8),
+            dma(PEERS), dma(PEERS), dma(PEERS), dma(PEERS), dma(7),
         ],
         compiler_params=pltpu.CompilerParams(
             vmem_limit_bytes=VMEM_BYTES, collective_id=1, has_side_effects=True
@@ -683,11 +678,11 @@
     )
     return pl.pallas_call(
         hand_over,
-        in_specs=[anywhere, anywhere],
+        in_specs=[vmem, vmem],
         out_specs=[anywhere, anywhere],
         out_shape=[shape((fields, blocks, cells), F32), shape((8, 512), F32)],
-        scratch_shapes=[buffer(fields, blocks, cells), buffer(8, 512), dma(fields + 1), dma(fields + 1)],
-        compiler_params=pltpu.CompilerParams(vmem_limit_bytes=VMEM_BYTES),
+        scratch_shapes=[dma(2)],
+        compiler_params=pltpu.CompilerParams(vmem_limit_bytes=4 * 1024 * 1024),
         name="hand_over",
     )(new_state, thread_temp)
 

time: 72.5 us -> 69.1 us (0.953)
  Pallas kernels: 71.3 us -> 67.6 us
    pallas_call x2, Pallas kernels: 71.3 us -> 67.6 us  [the longest x1 66.3 us: on_device(): pl.pallas_call(whole_kernel, in_specs=[pl.BlockSpec(memory_space=pltpu.HB...]
where the time goes in v4:
time: 69.1 us; the launch traced here: 68.4 us
  Pallas kernels  67.6 us (98%)
  between operations  0.8 us (1%)
    pallas_call x1, Pallas kernels, on_device(): pl.pallas_call(whole_kernel, in_specs=[pl.BlockSpec(memory_space=pltpu.HB...  66.3 us

profile of v4, /device:TPU:0, one launch (start us, length us, event | category | flops | bytes accessed | tf_op | source)
XLA Modules:
  0.0 68.4 jit_solution(10807814681139869844)
XLA Ops:
  0.6 66.3 %mhd_step.1 = (f32[8,128,512]{2,1,0:T(8,128)S(1)}, f32[8,512]{1,0:T(8,128)S(1)}) custom-call(f32[8,128,512]{2,1,0:T(8,128)} %state.1, f32[3,8,8,128]{3,2,1,0:T(8,128)} %jac_in.1, s32[4,2240]{1,0:T(4,128)} %send_in.1, s32[16,128]{1,0:T(8,128)} %bitcast.6, s32[32,128]{1,0:T(8,128)} %bitcast.4, s32[32,128]{1,0:T(8,128)} %bitcast.5, f32[256,512]{1,0:T(8,128)} %conductance.1, ...), custom_call_target="tpu_custom_call" | custom-call | tf_op jit(solution)/shard_map/mhd_step/pallas_call | solution.py:626
  66.9 1.3 %hand_over.1 = (f32[8,128,512]{2,1,0:T(8,128)}, f32[8,512]{1,0:T(8,128)}) custom-call(f32[8,128,512]{2,1,0:T(8,128)S(1)} %get-tuple-element.4.state, f32[8,512]{1,0:T(8,128)S(1)} %get-tuple-element.5.temp), custom_call_target="tpu_custom_call" | custom-call | tf_op jit(solution)/shard_map/hand_over/pallas_call | solution.py:679

commit v5 on v4

--- a/solution.py
+++ b/solution.py
@@ -54,6 +54,15 @@
     z = lax.rem(z + dz, 2)
     x = lax.rem(x + 4 + sign * dx, 4)
     return y * 8 + z * 4 + x
+
+
+def hops(n):
+    offset = 3 * n % PEERS
+    dy, dz, dx = offset // 8, offset // 4 % 2, offset % 4
+    return min(dy, 4 - dy) + 2 * dz + min(dx, 4 - dx)
+
+
+NEAR_FIRST = sorted(range(PEERS), key=hops)
 
 
 def column_plan(send, line, plan, cidx, copt, ccode):
@@ -502,17 +511,12 @@
     lax.fori_loop(1, PEERS, send_out, 0)
     arrived[0] = outgoing[me]
 
-    def prepare(i, carry):
-        for k in range(4):
-            lanes = slice(k * 512, (k + 1) * 512)
-            s = 4 * i + k
-            point = jnp.concatenate([noted[s, 2 + c : 3 + c, :] for c in range(4)], axis=1).astype(jnp.int32)
-            picks[i, :, lanes] = one_hot(iota((128, 512), 0) == (point & 127))
-            row = ((point >> 7) & 3) * 8 + (point >> 9)
-            rows_of[i, :, lanes] = jnp.broadcast_to(jnp.where(point < 0, -1, row), (8, 512))
-        return carry
-
-    lax.fori_loop(0, PEERS // 4, prepare, 0)
+    for place, n in enumerate(NEAR_FIRST):
+        i, lanes = place // 4, slice(place % 4 * 512, (place % 4 + 1) * 512)
+        point = jnp.concatenate([noted[n, 2 + c : 3 + c, :] for c in range(4)], axis=1).astype(jnp.int32)
+        picks[i, :, lanes] = one_hot(iota((128, 512), 0) == (point & 127))
+        row = ((point >> 7) & 3) * 8 + (point >> 9)
+        rows_of[i, :, lanes] = jnp.broadcast_to(jnp.where(point < 0, -1, row), (8, 512))
 
 
     def other_field(g, carry):
@@ -522,15 +526,14 @@
 
     lax.fori_loop(0, 3, other_field, 0)
 
-    def get_out(n, carry):
-        out_copy(n).wait()
-        return carry
-
-    lax.fori_loop(1, PEERS, get_out, 0)
     total = jnp.zeros((128, 64), F32)
     for i in range(PEERS // 4):
+        near = NEAR_FIRST[4 * i : 4 * i + 4]
+        for n in near:
+            if n:
+                out_copy(n).wait()
         mask = one_hot(iota((32, 2048), 0) == rows_of[i, 0:1, :])
-        line = jnp.concatenate([rows_to_lanes(arrived, 4 * i + k) for k in range(4)], axis=1)
+        line = jnp.concatenate([rows_to_lanes(arrived, n) for n in near], axis=1)
         high, low = high_low(line)
         rows = jnp.concatenate([mask * high.astype(BF16), mask * low.astype(BF16)], axis=0)
         total = total + lax.dot_general(
@@ -548,20 +551,18 @@
     high, low = high_low(solved)
     answers = jnp.concatenate(lanes_to_rows(high) + lanes_to_rows(low), axis=0).astype(BF16)
 
-    for i in range(PEERS // 4):
+    for i in reversed(range(PEERS // 4)):
         got = jnp.dot(answers, picks[i], preferred_element_type=F32)
         got = got[0:32] + got[32:64]
         mask = iota((32, 2048), 0) == rows_of[i, 0:1, :]
         line = jnp.sum(jnp.where(mask, got, 0.0), axis=0, keepdims=True)
         for k in range(4):
             part = lanes_to_rows(line[:, k * 512 : (k + 1) * 512])
-            back[4 * i + k] = jnp.concatenate(part + [jnp.zeros((4, 128), F32)], axis=0)
-
-    def send_back(n, carry):
-        back_copy(n).start()
-        return carry
-
-    lax.fori_loop(1, PEERS, send_back, 0)
+            n = NEAR_FIRST[4 * i + k]
+            back[n] = jnp.concatenate(part + [jnp.zeros((4, 128), F32)], axis=0)
+            if n:
+                back_copy(n).start()
+
     returned[0] = back[0]
 
     lax.fori_loop(3, 7, other_field, 0)

time: 69.1 us -> 66.7 us (0.965)
  Pallas kernels: 67.6 us -> 64.8 us
    pallas_call x1, Pallas kernels: 66.3 us -> 63.5 us  [on_device(): pl.pallas_call(whole_kernel, in_specs=[pl.BlockSpec(memory_space=pltpu.HB...]
where the time goes in v5:
time: 66.7 us; the launch traced here: 65.6 us
  Pallas kernels  64.8 us (97%)
  between operations  0.8 us (1%)
    pallas_call x1, Pallas kernels, on_device(): pl.pallas_call(whole_kernel, in_specs=[pl.BlockSpec(memory_space=pltpu.HB...  63.5 us
    pallas_call x1, Pallas kernels, on_device(): pl.pallas_call(hand_over, in_specs=[vmem, vmem], out_specs=[anywhere, any...  1.34 us

profile of v5, /device:TPU:0, one launch (start us, length us, event | category | flops | bytes accessed | tf_op | source)
XLA Modules:
  0.0 65.6 jit_solution(8766907681025687157)
XLA Ops:
  0.6 63.5 %mhd_step.1 = (f32[8,128,512]{2,1,0:T(8,128)S(1)}, f32[8,512]{1,0:T(8,128)S(1)}) custom-call(f32[8,128,512]{2,1,0:T(8,128)} %state.1, f32[3,8,8,128]{3,2,1,0:T(8,128)} %jac_in.1, s32[4,2240]{1,0:T(4,128)} %send_in.1, s32[16,128]{1,0:T(8,128)} %bitcast.6, s32[32,128]{1,0:T(8,128)} %bitcast.4, s32[32,128]{1,0:T(8,128)} %bitcast.5, f32[256,512]{1,0:T(8,128)} %conductance.1, ...), custom_call_target="tpu_custom_call" | custom-call | tf_op jit(solution)/shard_map/mhd_step/pallas_call | solution.py:627
  64.1 1.3 %hand_over.1 = (f32[8,128,512]{2,1,0:T(8,128)}, f32[8,512]{1,0:T(8,128)}) custom-call(f32[8,128,512]{2,1,0:T(8,128)S(1)} %get-tuple-element.4.state, f32[8,512]{1,0:T(8,128)S(1)} %get-tuple-element.5.temp), custom_call_target="tpu_custom_call" | custom-call | tf_op jit(solution)/shard_map/hand_over/pallas_call | solution.py:680
